TPU v7x, 32 devices: a whole 2x2x4 slice. The times are simulated.
32 devices in a mesh: rep: 8 (over z, y), shard: 4 (over x, core).
Axes of the slice: x: 2, y: 2, z: 4, core: 2. Of those that a mesh axis runs over, the one named last changes fastest.
Arguments:
- tokens: bfloat16 [8, 1024, 768], P('rep', 'shard'), may hold values from -6 to 6
- encoded: bfloat16 [8, 1024, 768], P('rep', 'shard'), may hold values from -6 to 6
- block_ids: int32 [8, 1024], P('rep', 'shard'), may hold values from 0 to 7, never falling along the last dimension, each value on 1 to 256 neighbouring positions
- buckets: int32 [2047], replicated, may hold values from 0 to 31
- cotangent: bfloat16 [8, 1024, 768], P('rep', 'shard'), may hold values from -6 to 6
- norm_self: bfloat16 [768], P('shard'), may hold values from 0.25 to 1.75
- self_query: bfloat16 [768, 768], P('shard'), may hold values from -0.02734375 to 0.02734375
- self_keyval: bfloat16 [2, 768, 768], P(None, 'shard'), may hold values from -0.21875 to 0.21875
- self_output: bfloat16 [768, 768], P('shard'), may hold values from -1.75 to 1.75
- bucket_bias: bfloat16 [12, 32], P(None, 'shard'), may hold values from -4 to 4
- norm_cross: bfloat16 [768], P('shard'), may hold values from 0.25 to 1.75
- cross_query: bfloat16 [768, 768], P('shard'), may hold values from -0.02734375 to 0.02734375
- cross_keyval: bfloat16 [2, 768, 768], P(None, 'shard'), may hold values from -0.21875 to 0.21875
- cross_output: bfloat16 [768, 768], P('shard'), may hold values from -1.75 to 1.75
- norm_feed: bfloat16 [768], P('shard'), may hold values from 0.25 to 1.75
- feed_in: bfloat16 [768, 3072], P('shard'), may hold values from -0.21875 to 0.21875
- feed_out: bfloat16 [3072, 768], P('shard'), may hold values from -0.15625 to 0.15625
Outputs:
- result: bfloat16 [8, 1024, 768], P('rep', 'shard')
- d_tokens: float32 [8, 1024, 768], P('rep', 'shard')
- d_encoded: float32 [8, 1024, 768], P('rep', 'shard')
- d_norm_self: float32 [768], P('shard')
- d_self_query: float32 [768, 768], P('shard')
- d_self_keyval: float32 [2, 768, 768], P(None, 'shard')
- d_self_output: float32 [768, 768], P('shard')
- d_bucket_bias: float32 [12, 32], P(None, 'shard')
- d_norm_cross: float32 [768], P('shard')
- d_cross_query: float32 [768, 768], P('shard')
- d_cross_keyval: float32 [2, 768, 768], P(None, 'shard')
- d_cross_output: float32 [768, 768], P('shard')
- d_norm_feed: float32 [768], P('shard')
- d_feed_in: float32 [768, 3072], P('shard')
- d_feed_out: float32 [3072, 768], P('shard')
Inputs may be any that keep to these rules, and one draw needn't show every extreme that they name: `block_ids`: never falls along a sequence; at most 256 positions of a sequence share a number. `buckets`: entry 1023 + k serves a key k positions after its query.
All inputs are finite; a program needn't handle non-finite values.
Results may differ from a plain program's by a relative error of at most 0.025.
Values may be sent and summed in bfloat16 or wider, within the bound.
A program may use at most 192 MiB of HBM per device.

v0:
```python
import jax
import jax.numpy as jnp
from jax import lax
from jax.sharding import PartitionSpec as P

H = 12


EPSILON = 1e-06
MASKED = -1e30
TOP_PRECISION = lax.Precision.HIGHEST


def normalize(values, gain):
    return values * lax.rsqrt(jnp.mean(values * values, axis=-1, keepdims=True) + EPSILON) * gain


def split_heads(values, head_count):
    return values.reshape(
        values.shape[0], values.shape[1], head_count, values.shape[2] // head_count
    )


def bucket_onehot(buckets, row_anchor, col_anchor, row_count, col_count, length, bucket_count):
    row_pos = row_anchor + jnp.arange(row_count, dtype=jnp.int32)
    col_pos = col_anchor + jnp.arange(col_count, dtype=jnp.int32)
    offsets = col_pos[None, :] - row_pos[:, None] + (length - 1)
    labels = jnp.take(buckets, offsets)
    return (labels[None, :, :] == jnp.arange(bucket_count, dtype=jnp.int32)[:, None, None]).astype(
        jnp.float32
    )


def skew_bias(relative_bias_matrix, indicator_matrix):
    return jnp.einsum(
        "id,duf->iuf",
        relative_bias_matrix.astype(jnp.float32),
        indicator_matrix,
        precision=TOP_PRECISION,
    )


def skew_fold(score_gradient, indicator_matrix):
    return jnp.einsum("pgw,igw->pi", score_gradient, indicator_matrix, precision=TOP_PRECISION)


def plain_adjust(scores, anchor):
    return scores


def attend(query_heads, key_rows, value_rows, score_correction, step_rows):
    groups, row_count, head_count, head_width = query_heads.shape
    block_count = key_rows.shape[1] // step_rows

    def scores_at(block_index):
        anchor = block_index * step_rows
        key_block = split_heads(
            lax.dynamic_slice_in_dim(key_rows, anchor, step_rows, 1), head_count
        )
        scores = jnp.einsum(
            "gqhd,gkhd->ghqk", query_heads, key_block, preferred_element_type=jnp.float32
        )
        return (score_correction(scores, anchor), anchor)

    def measure(running_state, block_index):
        running, summed = running_state
        scores, anchor = scores_at(block_index)
        newer = jnp.maximum(running, jnp.max(scores, axis=-1))
        summed = summed * jnp.exp(running - newer) + jnp.sum(
            jnp.exp(scores - newer[..., None]), axis=-1
        )
        return ((newer, summed), None)

    start_top = jnp.full((groups, head_count, row_count), MASKED, jnp.float32)
    indices = jnp.arange(block_count, dtype=jnp.int32)
    (running, summed), _ = lax.scan(measure, (start_top, jnp.zeros_like(start_top)), indices)
    logsum = running + jnp.log(summed)

    def collect(gathered_sum, block_index):
        scores, anchor = scores_at(block_index)
        weights = jnp.exp(scores - logsum[..., None]).astype(jnp.bfloat16)
        value_block = split_heads(
            lax.dynamic_slice_in_dim(value_rows, anchor, step_rows, 1), head_count
        )
        gathered_sum = gathered_sum + jnp.einsum(
            "ghqk,gkhd->gqhd", weights, value_block, preferred_element_type=jnp.float32
        )
        return (gathered_sum, None)

    gathered_sum, _ = lax.scan(
        collect, jnp.zeros((groups, row_count, head_count, head_width), jnp.float32), indices
    )
    return (gathered_sum.reshape(groups, row_count, head_count * head_width), logsum)


def attend_back(
    query_heads,
    key_rows,
    value_rows,
    score_correction,
    step_rows,
    logsum,
    output,
    grad_out,
    fold_bias,
    bias_start,
):
    groups, row_count, head_count, head_width = query_heads.shape
    length = key_rows.shape[1]
    model_width = head_count * head_width
    grad_heads = split_heads(grad_out, head_count)
    row_delta = jnp.swapaxes(
        jnp.sum(grad_heads.astype(jnp.float32) * split_heads(output, head_count), axis=-1), 1, 2
    )

    def visit(running_state, block_index):
        grad_query, grad_keys, grad_values, bias_sum = running_state
        anchor = block_index * step_rows
        key_block = split_heads(
            lax.dynamic_slice_in_dim(key_rows, anchor, step_rows, 1), head_count
        )
        value_block = split_heads(
            lax.dynamic_slice_in_dim(value_rows, anchor, step_rows, 1), head_count
        )
        scores = score_correction(
            jnp.einsum(
                "gqhd,gkhd->ghqk", query_heads, key_block, preferred_element_type=jnp.float32
            ),
            anchor,
        )
        weights = jnp.exp(scores - logsum[..., None])
        grad_weights = jnp.einsum(
            "gqhd,gkhd->ghqk", grad_heads, value_block, preferred_element_type=jnp.float32
        )
        score_gradient = weights * (grad_weights - row_delta[..., None])
        lowered = score_gradient.astype(jnp.bfloat16)
        grad_query = grad_query + jnp.einsum(
            "ghqk,gkhd->gqhd", lowered, key_block, preferred_element_type=jnp.float32
        )
        key_part = jnp.einsum(
            "ghqk,gqhd->gkhd", lowered, query_heads, preferred_element_type=jnp.float32
        ).reshape(groups, step_rows, model_width)
        value_part = jnp.einsum(
            "ghqk,gqhd->gkhd",
            weights.astype(jnp.bfloat16),
            grad_heads,
            preferred_element_type=jnp.float32,
        ).reshape(groups, step_rows, model_width)
        grad_keys = lax.dynamic_update_slice_in_dim(grad_keys, key_part, anchor, 1)
        grad_values = lax.dynamic_update_slice_in_dim(grad_values, value_part, anchor, 1)
        if fold_bias is not None:
            bias_sum = bias_sum + fold_bias(jnp.sum(score_gradient, axis=0), anchor)
        return ((grad_query, grad_keys, grad_values, bias_sum), None)

    start_state = (
        jnp.zeros((groups, row_count, head_count, head_width), jnp.float32),
        jnp.zeros((groups, length, model_width), jnp.float32),
        jnp.zeros((groups, length, model_width), jnp.float32),
        bias_start,
    )
    (grad_query, grad_keys, grad_values, bias_sum), _ = lax.scan(
        visit, start_state, jnp.arange(length // step_rows, dtype=jnp.int32)
    )
    return (grad_query.reshape(groups * row_count, model_width), grad_keys, grad_values, bias_sum)


def shards(
    tokens,
    encoded,
    block_ids,
    buckets,
    cotangent,
    norm_self,
    self_query,
    self_keyval,
    self_output,
    bucket_bias,
    norm_cross,
    cross_query,
    cross_keyval,
    cross_output,
    norm_feed,
    feed_in,
    feed_out,
):
    groups, positions, model_width = tokens.shape
    head_count = H
    length = (buckets.shape[0] + 1) // 2
    memory_local = encoded.shape[1]
    memory_len = memory_local * lax.axis_size("shard")
    key_step = min(512, length)
    memory_step = min(512, memory_len)
    row_anchor = lax.axis_index("shard") * positions
    count_rows = groups * positions
    inputs = tokens.astype(jnp.float32).reshape(count_rows, model_width)
    memory_rows = encoded.reshape(groups * memory_local, model_width)
    row_blocks = block_ids.astype(jnp.bfloat16)

    def to_heads(flat_rows):
        return split_heads(flat_rows.reshape(groups, positions, model_width), head_count)

    def self_adjust_for(relative_bias_matrix, blocks_whole):

        def score_correction(scores, anchor):
            indicator_matrix = bucket_onehot(
                buckets,
                row_anchor,
                anchor,
                positions,
                key_step,
                length,
                relative_bias_matrix.shape[1],
            )
            bias_block = skew_bias(relative_bias_matrix, indicator_matrix)
            key_blocks = lax.dynamic_slice_in_dim(blocks_whole, anchor, key_step, 1)
            allowed = key_blocks[:, None, :] <= row_blocks[:, :, None]
            return jnp.where(allowed[:, None], scores + bias_block[None], MASKED)

        return score_correction

    def self_fold_for(relative_bias_matrix):

        def fold_bias(score_gradient, anchor):
            indicator_matrix = bucket_onehot(
                buckets,
                row_anchor,
                anchor,
                positions,
                key_step,
                length,
                relative_bias_matrix.shape[1],
            )
            return skew_fold(score_gradient, indicator_matrix)

        return fold_bias

    gain_first, query_first, keyval_first, output_first, table_first = (
        lax.all_gather(norm_self, "shard", axis=0, tiled=True),
        lax.all_gather(self_query, "shard", axis=0, tiled=True),
        lax.all_gather(self_keyval, "shard", axis=1, tiled=True),
        lax.all_gather(self_output, "shard", axis=0, tiled=True),
        lax.all_gather(bucket_bias, "shard", axis=1, tiled=True),
    )
    normed_first = normalize(inputs, gain_first.astype(jnp.float32)).astype(jnp.bfloat16)
    query_local = jnp.dot(normed_first, query_first, preferred_element_type=jnp.float32).astype(
        jnp.bfloat16
    )
    pair_local = jnp.einsum(
        "rd,cde->cre", normed_first, keyval_first, preferred_element_type=jnp.float32
    ).astype(jnp.bfloat16)
    local_keys = pair_local[0].reshape(groups, positions, model_width)
    local_values = pair_local[1].reshape(groups, positions, model_width)
    keys_whole, values_whole, blocks_whole = (
        lax.all_gather(local_keys, "shard", axis=1, tiled=True),
        lax.all_gather(local_values, "shard", axis=1, tiled=True),
        lax.all_gather(row_blocks, "shard", axis=1, tiled=True),
    )
    attended_first, logsum_first = attend(
        to_heads(query_local),
        keys_whole,
        values_whole,
        self_adjust_for(table_first, blocks_whole),
        key_step,
    )
    first_reduced_copy = attended_first.reshape(count_rows, model_width).astype(jnp.bfloat16)
    first = inputs + jnp.dot(first_reduced_copy, output_first, preferred_element_type=jnp.float32)
    gain_second, query_second, keyval_second, output_second = (
        lax.all_gather(norm_cross, "shard", axis=0, tiled=True),
        lax.all_gather(cross_query, "shard", axis=0, tiled=True),
        lax.all_gather(cross_keyval, "shard", axis=1, tiled=True),
        lax.all_gather(cross_output, "shard", axis=0, tiled=True),
    )
    memory_key_value = jnp.einsum(
        "rd,cde->cre", memory_rows, keyval_second, preferred_element_type=jnp.float32
    ).astype(jnp.bfloat16)
    memory_keys = memory_key_value[0].reshape(groups, memory_local, model_width)
    memory_values = memory_key_value[1].reshape(groups, memory_local, model_width)
    memory_keys_whole, memory_values_whole = (
        lax.all_gather(memory_keys, "shard", axis=1, tiled=True),
        lax.all_gather(memory_values, "shard", axis=1, tiled=True),
    )
    normed_second = normalize(first, gain_second.astype(jnp.float32)).astype(jnp.bfloat16)
    query_cross = jnp.dot(normed_second, query_second, preferred_element_type=jnp.float32).astype(
        jnp.bfloat16
    )
    attended_second, logsum_second = attend(
        to_heads(query_cross), memory_keys_whole, memory_values_whole, plain_adjust, memory_step
    )
    lowered_second = attended_second.reshape(count_rows, model_width).astype(jnp.bfloat16)
    second = first + jnp.dot(lowered_second, output_second, preferred_element_type=jnp.float32)
    gain_third, inner_weight, outer_weight = (
        lax.all_gather(norm_feed, "shard", axis=0, tiled=True),
        lax.all_gather(feed_in, "shard", axis=0, tiled=True),
        lax.all_gather(feed_out, "shard", axis=0, tiled=True),
    )
    normed_third = normalize(second, gain_third.astype(jnp.float32)).astype(jnp.bfloat16)
    preact = jnp.dot(normed_third, inner_weight, preferred_element_type=jnp.float32)
    activated, gelu_back = jax.vjp(jax.nn.gelu, preact)
    hidden = activated.astype(jnp.bfloat16)
    outcome = (second + jnp.dot(hidden, outer_weight, preferred_element_type=jnp.float32)).astype(
        jnp.bfloat16
    )
    fetched = (
        lax.all_gather(norm_self, "shard", axis=0, tiled=True),
        lax.all_gather(self_query, "shard", axis=0, tiled=True),
        lax.all_gather(self_keyval, "shard", axis=1, tiled=True),
        lax.all_gather(self_output, "shard", axis=0, tiled=True),
        lax.all_gather(bucket_bias, "shard", axis=1, tiled=True),
        lax.all_gather(norm_cross, "shard", axis=0, tiled=True),
        lax.all_gather(cross_query, "shard", axis=0, tiled=True),
        lax.all_gather(cross_keyval, "shard", axis=1, tiled=True),
        lax.all_gather(cross_output, "shard", axis=0, tiled=True),
        lax.all_gather(norm_feed, "shard", axis=0, tiled=True),
        lax.all_gather(feed_in, "shard", axis=0, tiled=True),
        lax.all_gather(feed_out, "shard", axis=0, tiled=True),
        lax.all_gather(local_keys, "shard", axis=1, tiled=True),
        lax.all_gather(local_values, "shard", axis=1, tiled=True),
        lax.all_gather(row_blocks, "shard", axis=1, tiled=True),
        lax.all_gather(memory_keys, "shard", axis=1, tiled=True),
        lax.all_gather(memory_values, "shard", axis=1, tiled=True),
    )
    (
        gain_first,
        query_first,
        keyval_first,
        output_first,
        table_first,
        gain_second,
        query_second,
        keyval_second,
        output_second,
        gain_third,
        inner_weight,
        outer_weight,
        keys_whole,
        values_whole,
        blocks_whole,
        memory_keys_whole,
        memory_values_whole,
    ) = fetched
    grad_result = cotangent.reshape(count_rows, model_width)
    grad_top = grad_result.astype(jnp.float32)
    d_outer = jnp.einsum("rf,rd->fd", hidden, grad_result, preferred_element_type=jnp.float32)
    grad_hidden = jnp.einsum(
        "rd,fd->rf", grad_result, outer_weight, preferred_element_type=jnp.float32
    )
    grad_preact = gelu_back(grad_hidden)[0].astype(jnp.bfloat16)
    d_inner = jnp.einsum("rd,rf->df", normed_third, grad_preact, preferred_element_type=jnp.float32)
    grad_normed_third = jnp.einsum(
        "rf,df->rd", grad_preact, inner_weight, preferred_element_type=jnp.float32
    )
    _, pullback_third = jax.vjp(normalize, second, gain_third.astype(jnp.float32))
    back_second, d_gain_third = pullback_third(grad_normed_third)
    grad_second = grad_top + back_second
    feed_shares = (
        lax.psum_scatter(
            d_gain_third.astype(jnp.bfloat16), "shard", scatter_dimension=0, tiled=True
        ).astype(jnp.float32),
        lax.psum_scatter(
            d_inner.astype(jnp.bfloat16), "shard", scatter_dimension=0, tiled=True
        ).astype(jnp.float32),
        lax.psum_scatter(
            d_outer.astype(jnp.bfloat16), "shard", scatter_dimension=0, tiled=True
        ).astype(jnp.float32),
    )
    second_reduced_gradient = grad_second.astype(jnp.bfloat16)
    d_output_second = jnp.einsum(
        "rd,re->de", lowered_second, second_reduced_gradient, preferred_element_type=jnp.float32
    )
    grad_att_second = (
        jnp.einsum(
            "re,de->rd", second_reduced_gradient, output_second, preferred_element_type=jnp.float32
        )
        .astype(jnp.bfloat16)
        .reshape(groups, positions, model_width)
    )
    grad_query_cross, grad_keys_part, grad_values_part, _ = attend_back(
        to_heads(query_cross),
        memory_keys_whole,
        memory_values_whole,
        plain_adjust,
        memory_step,
        logsum_second,
        attended_second,
        grad_att_second,
        None,
        jnp.zeros((1,), jnp.float32),
    )
    grad_memory_keys, grad_memory_values = (
        lax.psum_scatter(
            grad_keys_part.astype(jnp.bfloat16), "shard", scatter_dimension=1, tiled=True
        ).astype(jnp.float32),
        lax.psum_scatter(
            grad_values_part.astype(jnp.bfloat16), "shard", scatter_dimension=1, tiled=True
        ).astype(jnp.float32),
    )
    grad_memory_pair = jnp.stack(
        [
            grad_memory_keys.reshape(groups * memory_local, model_width),
            grad_memory_values.reshape(groups * memory_local, model_width),
        ]
    ).astype(jnp.bfloat16)
    d_keyval_second = jnp.einsum(
        "rd,cre->cde", memory_rows, grad_memory_pair, preferred_element_type=jnp.float32
    )
    d_memory = jnp.einsum(
        "cre,cde->rd", grad_memory_pair, keyval_second, preferred_element_type=jnp.float32
    )
    grad_query_low = grad_query_cross.astype(jnp.bfloat16)
    d_query_second = jnp.einsum(
        "rd,re->de", normed_second, grad_query_low, preferred_element_type=jnp.float32
    )
    grad_normed_second = jnp.einsum(
        "re,de->rd", grad_query_low, query_second, preferred_element_type=jnp.float32
    )
    _, pullback_second = jax.vjp(normalize, first, gain_second.astype(jnp.float32))
    back_first, d_gain_second = pullback_second(grad_normed_second)
    grad_first = grad_second + back_first
    cross_shares = (
        lax.psum_scatter(
            d_gain_second.astype(jnp.bfloat16), "shard", scatter_dimension=0, tiled=True
        ).astype(jnp.float32),
        lax.psum_scatter(
            d_query_second.astype(jnp.bfloat16), "shard", scatter_dimension=0, tiled=True
        ).astype(jnp.float32),
        lax.psum_scatter(
            d_keyval_second.astype(jnp.bfloat16), "shard", scatter_dimension=1, tiled=True
        ).astype(jnp.float32),
        lax.psum_scatter(
            d_output_second.astype(jnp.bfloat16), "shard", scatter_dimension=0, tiled=True
        ).astype(jnp.float32),
    )
    grad_first_low = grad_first.astype(jnp.bfloat16)
    d_output_first = jnp.einsum(
        "rd,re->de", first_reduced_copy, grad_first_low, preferred_element_type=jnp.float32
    )
    grad_att_first = (
        jnp.einsum("re,de->rd", grad_first_low, output_first, preferred_element_type=jnp.float32)
        .astype(jnp.bfloat16)
        .reshape(groups, positions, model_width)
    )
    bias_start = jnp.zeros(table_first.shape, jnp.float32)
    grad_query_self, grad_keys_self_part, grad_values_self_part, d_table = attend_back(
        to_heads(query_local),
        keys_whole,
        values_whole,
        self_adjust_for(table_first, blocks_whole),
        key_step,
        logsum_first,
        attended_first,
        grad_att_first,
        self_fold_for(table_first),
        bias_start,
    )
    grad_keys_self, grad_values_self = (
        lax.psum_scatter(
            grad_keys_self_part.astype(jnp.bfloat16), "shard", scatter_dimension=1, tiled=True
        ).astype(jnp.float32),
        lax.psum_scatter(
            grad_values_self_part.astype(jnp.bfloat16), "shard", scatter_dimension=1, tiled=True
        ).astype(jnp.float32),
    )
    grad_pair_low = jnp.stack(
        [
            grad_keys_self.reshape(count_rows, model_width),
            grad_values_self.reshape(count_rows, model_width),
        ]
    ).astype(jnp.bfloat16)
    grad_query_self_low = grad_query_self.astype(jnp.bfloat16)
    d_query_first = jnp.einsum(
        "rd,re->de", normed_first, grad_query_self_low, preferred_element_type=jnp.float32
    )
    d_keyval_first = jnp.einsum(
        "rd,cre->cde", normed_first, grad_pair_low, preferred_element_type=jnp.float32
    )
    grad_normed_first = jnp.einsum(
        "re,de->rd", grad_query_self_low, query_first, preferred_element_type=jnp.float32
    ) + jnp.einsum("cre,cde->rd", grad_pair_low, keyval_first, preferred_element_type=jnp.float32)
    _, pullback_first = jax.vjp(normalize, inputs, gain_first.astype(jnp.float32))
    back_inputs, d_gain_first = pullback_first(grad_normed_first)
    d_inputs = grad_first + back_inputs
    self_shares = (
        lax.psum_scatter(
            d_gain_first.astype(jnp.bfloat16), "shard", scatter_dimension=0, tiled=True
        ).astype(jnp.float32),
        lax.psum_scatter(
            d_query_first.astype(jnp.bfloat16), "shard", scatter_dimension=0, tiled=True
        ).astype(jnp.float32),
        lax.psum_scatter(
            d_keyval_first.astype(jnp.bfloat16), "shard", scatter_dimension=1, tiled=True
        ).astype(jnp.float32),
        lax.psum_scatter(
            d_output_first.astype(jnp.bfloat16), "shard", scatter_dimension=0, tiled=True
        ).astype(jnp.float32),
        lax.psum_scatter(
            d_table.astype(jnp.bfloat16), "shard", scatter_dimension=1, tiled=True
        ).astype(jnp.float32),
    )
    totals = (
        lax.psum(self_shares[0].astype(jnp.bfloat16), "rep").astype(jnp.float32),
        lax.psum(self_shares[1].astype(jnp.bfloat16), "rep").astype(jnp.float32),
        lax.psum(self_shares[2].astype(jnp.bfloat16), "rep").astype(jnp.float32),
        lax.psum(self_shares[3].astype(jnp.bfloat16), "rep").astype(jnp.float32),
        lax.psum(self_shares[4].astype(jnp.bfloat16), "rep").astype(jnp.float32),
        lax.psum(cross_shares[0].astype(jnp.bfloat16), "rep").astype(jnp.float32),
        lax.psum(cross_shares[1].astype(jnp.bfloat16), "rep").astype(jnp.float32),
        lax.psum(cross_shares[2].astype(jnp.bfloat16), "rep").astype(jnp.float32),
        lax.psum(cross_shares[3].astype(jnp.bfloat16), "rep").astype(jnp.float32),
        lax.psum(feed_shares[0].astype(jnp.bfloat16), "rep").astype(jnp.float32),
        lax.psum(feed_shares[1].astype(jnp.bfloat16), "rep").astype(jnp.float32),
        lax.psum(feed_shares[2].astype(jnp.bfloat16), "rep").astype(jnp.float32),
    )
    return (
        outcome.reshape(groups, positions, model_width),
        d_inputs.reshape(groups, positions, model_width),
        d_memory.reshape(groups, memory_local, model_width),
        totals[0],
        totals[1],
        totals[2],
        totals[3],
        totals[4],
        totals[5],
        totals[6],
        totals[7],
        totals[8],
        totals[9],
        totals[10],
        totals[11],
    )


def solution(mesh):
    placed = (
        P("rep", "shard", None),
        P("rep", "shard", None),
        P("rep", "shard"),
        P(),
        P("rep", "shard", None),
        P("shard"),
        P("shard", None),
        P(None, "shard", None),
        P("shard", None),
        P(None, "shard"),
        P("shard"),
        P("shard", None),
        P(None, "shard", None),
        P("shard", None),
        P("shard"),
        P("shard", None),
        P("shard", None),
    )
    return jax.shard_map(
        shards,
        mesh=mesh,
        in_specs=placed,
        out_specs=(
            P("rep", "shard", None),
            P("rep", "shard", None),
            P("rep", "shard", None),
            P("shard"),
            P("shard", None),
            P(None, "shard", None),
            P("shard", None),
            P(None, "shard"),
            P("shard"),
            P("shard", None),
            P(None, "shard", None),
            P("shard", None),
            P("shard"),
            P("shard", None),
            P("shard", None),
        ),
        check_vma=False,
    )
```

profile of v0, /device:TPU:0, one launch (start us, length us, event | category | flops | bytes accessed | tf_op | source)
XLA Modules:
  0.0 5465.8 jit_solution(2638374843560503870)
XLA Ops:
  14.0 8.5 all-reduce.12
  24.2 12.3 all-gather.13.cloned.1.call-done
  42.0 20.1 all-gather.23.cloned.1.call-done
  84.3 18.7 all-gather.17.cloned.1.call-done
  106.1 1511.3 %while.80 = (s32[]{:T(128)}, f32[1,12,256]{2,1,0:T(8,128)}, f32[1,12,256]{2,1,0:T(8,128)}, s32[2]{0:T(128)}, bf16[1,1024]{1,0:T(2,128)(2,1)}, /*index=5*/bf16[1,...) while((s32[]{:T(128)}, f32[1,12,256]{2,1,0:T(8,128)}, ...), condition=%wide.region_4.6_spmd.clone, body=%wide.region_1.5_spmd.clone.sunk | while | flops 316161792 | bytes 49512228 | solution.py:76
  109.0 724.9 %gather_fusion = s32[131072]{0:T(1024)S(1)} fusion(s32[2047]{0:T(1024)S(1)} %get-tuple-element.1466, s32[131072]{0:T(1024)S(1)} %broadcast_clamp_fusion.6), kind=kCustom, calls=%fused_computation.clone.clone.1 | custom fusion | bytes 1572864 | tf_op jit(solution)/shard_map/while/body/eval_jaxpr/jit(_take)/gather | solution.py:28
  840.2 9.2 copy.190
  850.8 6.6 fusion.250
  864.7 724.9 %gather_fusion = s32[131072]{0:T(1024)S(1)} fusion(s32[2047]{0:T(1024)S(1)} %get-tuple-element.1466, s32[131072]{0:T(1024)S(1)} %broadcast_clamp_fusion.6), kind=kCustom, calls=%fused_computation.clone.clone.1 | custom fusion | bytes 1572864 | tf_op jit(solution)/shard_map/while/body/eval_jaxpr/jit(_take)/gather | solution.py:28
  1595.8 9.2 copy.190
  1606.4 6.6 fusion.250
  1621.8 1504.0 %while.81 = (s32[]{:T(128)}, f32[1,256,12,64]{1,3,2,0:T(8,128)}, s32[2]{0:T(128)}, bf16[1,1024,768]{1,2,0:T(8,128)(2,1)}, bf16[1,1024]{1,0:T(2,128)(2,1)}, /*ind...) while((s32[]{:T(128)}, f32[1,256,12,64]{1,3,2,0:T(8,128)}, ...), condition=%wide.region_6.8_spmd.clone, body=%wide.region_5.7_spmd.clone.sunk | while | flops 516293376 | bytes 46907180 | solution.py:90
  1627.3 724.9 %gather_fusion.1 = s32[131072]{0:T(1024)S(1)} fusion(s32[2047]{0:T(1024)S(1)} %get-tuple-element.1516, s32[131072]{0:T(1024)S(1)} %broadcast_clamp_fusion.7), kind=kCustom, calls=%fused_computation.1.clone.clone.1 | custom fusion | bytes 1572864 | tf_op jit(solution)/shard_map/while/body/eval_jaxpr/jit(_take)/gather | solution.py:28
  2358.4 9.3 copy.192
  2379.1 724.9 %gather_fusion.1 = s32[131072]{0:T(1024)S(1)} fusion(s32[2047]{0:T(1024)S(1)} %get-tuple-element.1516, s32[131072]{0:T(1024)S(1)} %broadcast_clamp_fusion.7), kind=kCustom, calls=%fused_computation.1.clone.clone.1 | custom fusion | bytes 1572864 | tf_op jit(solution)/shard_map/while/body/eval_jaxpr/jit(_take)/gather | solution.py:28
  3110.3 9.3 copy.192
  3119.8 6.0 fusion.259
  3131.4 19.4 while.82
  3150.9 12.2 while.83
  3172.1 6.8 fusion.96
  3187.5 50.1 while.84
  3246.9 1580.7 %while.85 = (s32[]{:T(128)}, f32[1,256,12,64]{1,3,2,0:T(8,128)}, bf16[1,1024,768]{2,1,0:T(8,128)(2,1)}, bf16[1,1024,768]{2,1,0:T(8,128)(2,1)}, f32[12,32]{1,0:T(...) while((s32[]{:T(128)}, f32[1,256,12,64]{1,3,2,0:T(8,128)}, ...), condition=%wide.region_22.24_spmd.clone, body=%wide.region_21.23_spmd.clone.sunk | while | flops 1734739456 | bytes 169012416 | solution.py:161
  3252.0 724.9 %gather_fusion.2 = s32[131072]{0:T(1024)S(1)} fusion(s32[2047]{0:T(1024)S(1)} %get-tuple-element.1687, s32[131072]{0:T(1024)S(1)} %broadcast_clamp_fusion.8), kind=kCustom, calls=%fused_computation.2.clone.clone.1 | custom fusion | bytes 1572864 | tf_op jit(solution)/shard_map/while/body/eval_jaxpr/jit(_take)/gather | solution.py:28
  3983.1 9.2 copy.196
  4015.9 9.7 copy.199
  4025.6 11.1 fusion.299
  4042.1 724.9 %gather_fusion.2 = s32[131072]{0:T(1024)S(1)} fusion(s32[2047]{0:T(1024)S(1)} %get-tuple-element.1687, s32[131072]{0:T(1024)S(1)} %broadcast_clamp_fusion.8), kind=kCustom, calls=%fused_computation.2.clone.clone.1 | custom fusion | bytes 1572864 | tf_op jit(solution)/shard_map/while/body/eval_jaxpr/jit(_take)/gather | solution.py:28
  4773.3 9.2 copy.196
  4806.1 9.7 copy.199
  4815.8 11.1 fusion.299
  4829.5 26.5 reduce-scatter.11.cloned.1.call-done
  4857.0 29.7 reduce-scatter.13.cloned.1.call-done
  4890.1 6.9 copy.144
  4897.0 20.3 reduce-scatter.15.cloned.1.call-done
  4918.3 29.7 reduce-scatter.17.cloned.1.call-done
  4951.4 6.9 copy.147
  4974.7 6.4 convolution_convert_fusion
  4982.0 70.7 %all-reduce.19.cloned.1.call-done = (bf16[2,768,768]{2,0,1:T(2,128)(2,1)}, bf16[2,768,768]{2,0,1:T(2,128)(2,1)}) async-done(((bf16[2,768,768]{2,0,1:T(2,128)(2,1)}, bf16[2,768,768]{2,0,1:T(2,128)(2,1)}), (bf16[2,768,768]{2,0,1:T(2,128)(2,1)}, bf16[2,768,768]{2,0,1:T(2,128)(2,1)})) %all-reduce.19.cloned.1.call-update) | async-done | bytes 4718608
  5055.7 25.8 reduce-scatter.19.cloned.1.call-done
  5081.6 29.1 reduce-scatter.21.cloned.1.call-done
  5110.6 28.8 reduce-scatter.23.cloned.1.call-done
  5139.4 28.5 reduce-scatter.25.cloned.1.call-done
  5167.9 50.4 reduce-scatter.27.cloned.1.call-done
  5218.3 50.6 reduce-scatter.29.cloned.1.call-done
  5269.7 6.1 fusion.100
  5278.4 11.5 all-reduce.11
  5290.1 22.4 all-reduce.9
  5319.9 126.5 %all-reduce.17.cloned.1.call-done = (bf16[2,192,768]{2,0,1:T(2,128)(2,1)}, bf16[2,192,768]{2,0,1:T(2,128)(2,1)}, bf16[192,768]{1,0:T(8,128)(2,1)}, bf16[192,768]...) async-done(((bf16[2,192,768]{2,0,1:T(2,128)(2,1)}, ...) | async-done | bytes 4718608 | tf_op jit(solution)/shard_map/psum | solution.py:502
  (637 shorter events, 328.8 us)
Async XLA Ops:
  7.2 29.3 all-gather.13.cloned.1.call-start
  7.9 54.2 all-gather.23.cloned.1.call-start
  8.7 72.9 %all-gather.19.cloned.1.call-start = ((), (), s32[]{:S(2)}) async-start(), calls=%async_computation.13 | async-start | bytes 1474560 | tf_op jit(solution)/shard_map/all_gather | solution.py:239
  9.4 93.5 %all-gather.17.cloned.1.call-start = ((), (), s32[]{:S(2)}) async-start(), calls=%async_computation.12 | async-start | bytes 1966080 | tf_op jit(solution)/shard_map/all_gather | solution.py:254
  40.1 1578.6 %all-gather.15.cloned.1.call-start = ((), (), s32[]{:S(2)}) async-start(), calls=%async_computation.11 | async-start | bytes 1966080 | tf_op jit(solution)/shard_map/all_gather | solution.py:255
  40.7 3086.4 %all-gather.21.cloned.1.call-start = ((), (), s32[]{:S(2)}) async-start(), calls=%async_computation.14 | async-start | bytes 1474560 | tf_op jit(solution)/shard_map/all_gather | solution.py:241
  41.3 3087.9 %all-gather.29.cloned.1.call-start = ((), (), s32[]{:S(2)}) async-start(), calls=%async_computation.18 | async-start | bytes 1474560 | tf_op jit(solution)/shard_map/all_gather | solution.py:269
  42.0 3089.4 %all-gather.27.cloned.1.call-start = ((), (), s32[]{:S(2)}) async-start(), calls=%async_computation.17 | async-start | bytes 1966080 | tf_op jit(solution)/shard_map/all_gather | solution.py:279
  65.6 3085.3 %all-gather.25.cloned.1.call-start = ((), (), s32[]{:S(2)}) async-start(), calls=%async_computation.16 | async-start | bytes 1966080 | tf_op jit(solution)/shard_map/all_gather | solution.py:280
  66.4 3098.0 %all-gather.31.cloned.1.call-start = ((), (), s32[]{:S(2)}) async-start(), calls=%async_computation.19 | async-start | bytes 1474560 | tf_op jit(solution)/shard_map/all_gather | solution.py:271
  67.0 3099.5 %all-gather.33.cloned.1.call-start = ((), (), s32[]{:S(2)}) async-start(), calls=%async_computation.20 | async-start | bytes 5898240 | tf_op jit(solution)/shard_map/all_gather | solution.py:293
  67.7 3104.4 %all-gather.35.cloned.1.call-start = ((), (), s32[]{:S(2)}) async-start(), calls=%async_computation.21 | async-start | bytes 5898240 | tf_op jit(solution)/shard_map/all_gather | solution.py:294
  68.3 4787.7 %reduce-scatter.11.cloned.1.call-start = ((), (), s32[]{:S(2)}) async-start(), calls=%async_computation.22 | async-start | bytes 1966080 | tf_op jit(solution)/shard_map/reduce_scatter | solution.py:456
  109.0 725.0 %copy-start.69 = (s32[512]{0:T(512)S(1)}, s32[512]{0:T(512)}, u32[]{:S(2)}) copy-start(s32[512]{0:T(512)} %copy-done.68) | copy-start | bytes 6148 | tf_op jit(solution)/shard_map/while
  109.0 725.0 %copy-start.88 = (s32[256]{0:T(256)S(1)}, s32[256]{0:T(256)}, u32[]{:S(2)}) copy-start(s32[256]{0:T(256)} %copy-done.87) | copy-start | bytes 3076 | tf_op jit(solution)/shard_map/while
  109.0 725.2 %copy-start.52 = (bf16[12,32]{1,0:T(8,128)(2,1)S(1)}, bf16[12,32]{1,0:T(8,128)(2,1)}, u32[]{:S(2)}) copy-start(bf16[12,32]{1,0:T(8,128)(2,1)} %get-tuple-element.1467) | copy-start | bytes 2308 | tf_op jit(solution)/shard_map/while
  864.6 725.0 %copy-start.69 = (s32[512]{0:T(512)S(1)}, s32[512]{0:T(512)}, u32[]{:S(2)}) copy-start(s32[512]{0:T(512)} %copy-done.68) | copy-start | bytes 6148 | tf_op jit(solution)/shard_map/while
  864.6 725.0 %copy-start.88 = (s32[256]{0:T(256)S(1)}, s32[256]{0:T(256)}, u32[]{:S(2)}) copy-start(s32[256]{0:T(256)} %copy-done.87) | copy-start | bytes 3076 | tf_op jit(solution)/shard_map/while
  864.6 725.2 %copy-start.52 = (bf16[12,32]{1,0:T(8,128)(2,1)S(1)}, bf16[12,32]{1,0:T(8,128)(2,1)}, u32[]{:S(2)}) copy-start(bf16[12,32]{1,0:T(8,128)(2,1)} %get-tuple-element.1467) | copy-start | bytes 2308 | tf_op jit(solution)/shard_map/while
  1621.8 1505.3 %copy-start.25 = (bf16[1,256,768]{2,1,0:T(8,128)(2,1)S(1)}, bf16[1,256,768]{2,1,0:T(8,128)(2,1)}, u32[]{:S(2)}) copy-start(bf16[1,256,768]{2,1,0:T(8,128)(2,1)} %param.31) | copy-start | bytes 1179652
  1627.2 725.0 %copy-start.65 = (s32[512]{0:T(512)S(1)}, s32[512]{0:T(512)}, u32[]{:S(2)}) copy-start(s32[512]{0:T(512)} %copy-done.64) | copy-start | bytes 6148 | tf_op jit(solution)/shard_map/while
  1627.3 725.0 %copy-start.90 = (s32[256]{0:T(256)S(1)}, s32[256]{0:T(256)}, u32[]{:S(2)}) copy-start(s32[256]{0:T(256)} %copy-done.89) | copy-start | bytes 3076 | tf_op jit(solution)/shard_map/while
  1627.3 725.2 %copy-start.53 = (bf16[12,32]{1,0:T(8,128)(2,1)S(1)}, bf16[12,32]{1,0:T(8,128)(2,1)}, u32[]{:S(2)}) copy-start(bf16[12,32]{1,0:T(8,128)(2,1)} %get-tuple-element.1517) | copy-start | bytes 2308 | tf_op jit(solution)/shard_map/while
  2379.1 725.0 %copy-start.65 = (s32[512]{0:T(512)S(1)}, s32[512]{0:T(512)}, u32[]{:S(2)}) copy-start(s32[512]{0:T(512)} %copy-done.64) | copy-start | bytes 6148 | tf_op jit(solution)/shard_map/while
  2379.1 725.0 %copy-start.90 = (s32[256]{0:T(256)S(1)}, s32[256]{0:T(256)}, u32[]{:S(2)}) copy-start(s32[256]{0:T(256)} %copy-done.89) | copy-start | bytes 3076 | tf_op jit(solution)/shard_map/while
  2379.1 725.2 %copy-start.53 = (bf16[12,32]{1,0:T(8,128)(2,1)S(1)}, bf16[12,32]{1,0:T(8,128)(2,1)}, u32[]{:S(2)}) copy-start(bf16[12,32]{1,0:T(8,128)(2,1)} %get-tuple-element.1517) | copy-start | bytes 2308 | tf_op jit(solution)/shard_map/while
  3129.1 112.8 %copy-start.102 = (f32[256]{0:T(256)}, f32[256]{0:T(256)S(1)}, u32[]{:S(2)}) copy-start(f32[256]{0:T(256)S(1)} %fusion.135) | copy-start | bytes 3076
  3251.9 725.0 %copy-start.67 = (s32[512]{0:T(512)S(1)}, s32[512]{0:T(512)}, u32[]{:S(2)}) copy-start(s32[512]{0:T(512)} %copy-done.66) | copy-start | bytes 6148 | tf_op jit(solution)/shard_map/while
  3251.9 725.0 %copy-start.92 = (s32[256]{0:T(256)S(1)}, s32[256]{0:T(256)}, u32[]{:S(2)}) copy-start(s32[256]{0:T(256)} %copy-done.91) | copy-start | bytes 3076 | tf_op jit(solution)/shard_map/while
  3251.9 725.2 %copy-start.54 = (bf16[12,32]{1,0:T(8,128)(2,1)S(1)}, bf16[12,32]{1,0:T(8,128)(2,1)}, u32[]{:S(2)}) copy-start(bf16[12,32]{1,0:T(8,128)(2,1)} %get-tuple-element.1688) | copy-start | bytes 2308 | tf_op jit(solution)/shard_map/while
  4042.1 725.0 %copy-start.67 = (s32[512]{0:T(512)S(1)}, s32[512]{0:T(512)}, u32[]{:S(2)}) copy-start(s32[512]{0:T(512)} %copy-done.66) | copy-start | bytes 6148 | tf_op jit(solution)/shard_map/while
  4042.1 725.0 %copy-start.92 = (s32[256]{0:T(256)S(1)}, s32[256]{0:T(256)}, u32[]{:S(2)}) copy-start(s32[256]{0:T(256)} %copy-done.91) | copy-start | bytes 3076 | tf_op jit(solution)/shard_map/while
  4042.1 725.2 %copy-start.54 = (bf16[12,32]{1,0:T(8,128)(2,1)S(1)}, bf16[12,32]{1,0:T(8,128)(2,1)}, u32[]{:S(2)}) copy-start(bf16[12,32]{1,0:T(8,128)(2,1)} %get-tuple-element.1688) | copy-start | bytes 2308 | tf_op jit(solution)/shard_map/while
  4827.7 59.1 %reduce-scatter.13.cloned.1.call-start = ((), (), s32[]{:S(2)}) async-start(), calls=%async_computation.23 | async-start | bytes 1966080 | tf_op jit(solution)/shard_map/reduce_scatter | solution.py:459
  4827.7 60.0 %copy-start.26 = (bf16[1,256,768]{2,1,0:T(8,128)(2,1)S(1)}, bf16[1,256,768]{2,1,0:T(8,128)(2,1)}, u32[]{:S(2)}) copy-start(bf16[1,256,768]{2,1,0:T(8,128)(2,1)} %param.31) | copy-start | bytes 1179652
  4827.8 60.0 %copy-start.94 = (f32[768]{0:T(1024)S(1)}, f32[768]{0:T(1024)}, u32[]{:S(2)}) copy-start(f32[768]{0:T(1024)} %copy-done.93) | copy-start | bytes 9220
  4827.8 60.0 %copy-start.100 = (f32[256]{0:T(256)S(1)}, f32[256]{0:T(256)}, u32[]{:S(2)}) copy-start(f32[256]{0:T(256)} %copy-done.99) | copy-start | bytes 3076
  4828.3 89.1 %reduce-scatter.15.cloned.1.call-start = ((), (), s32[]{:S(2)}) async-start(), calls=%async_computation.24 | async-start | bytes 1966080 | tf_op jit(solution)/shard_map/reduce_scatter | solution.py:390
  4828.9 119.2 %reduce-scatter.17.cloned.1.call-start = ((), (), s32[]{:S(2)}) async-start(), calls=%async_computation.25 | async-start | bytes 1966080 | tf_op jit(solution)/shard_map/reduce_scatter | solution.py:393
  4829.4 223.2 %all-reduce.19.cloned.1.call-start = ((), (), s32[]{:S(2)}) async-start(), calls=%async_computation.33 | async-start | bytes 9437184
  4958.3 123.3 %reduce-scatter.19.cloned.1.call-start = ((), (), s32[]{:S(2)}) async-start(), calls=%async_computation.26 | async-start | bytes 1474560 | tf_op jit(solution)/shard_map/reduce_scatter | solution.py:486
  4961.1 149.6 %reduce-scatter.21.cloned.1.call-start = ((), (), s32[]{:S(2)}) async-start(), calls=%async_computation.27 | async-start | bytes 1474560 | tf_op jit(solution)/shard_map/reduce_scatter | solution.py:492
  4962.7 176.7 %reduce-scatter.23.cloned.1.call-start = ((), (), s32[]{:S(2)}) async-start(), calls=%async_computation.28 | async-start | bytes 1474560 | tf_op jit(solution)/shard_map/reduce_scatter | solution.py:423
  4965.6 202.3 %reduce-scatter.25.cloned.1.call-start = ((), (), s32[]{:S(2)}) async-start(), calls=%async_computation.29 | async-start | bytes 1474560 | tf_op jit(solution)/shard_map/reduce_scatter | solution.py:429
  4968.4 249.9 %reduce-scatter.27.cloned.1.call-start = ((), (), s32[]{:S(2)}) async-start(), calls=%async_computation.30 | async-start | bytes 5898240 | tf_op jit(solution)/shard_map/reduce_scatter | solution.py:359
  4973.7 295.2 %reduce-scatter.29.cloned.1.call-start = ((), (), s32[]{:S(2)}) async-start(), calls=%async_computation.31 | async-start | bytes 5898240 | tf_op jit(solution)/shard_map/reduce_scatter | solution.py:362
  4981.1 465.4 %all-reduce.17.cloned.1.call-start = ((), (), s32[]{:S(2)}) async-start(), calls=%async_computation.32 | async-start | bytes 9437184 | tf_op jit(solution)/shard_map/psum | solution.py:502
  5052.6 216.9 %copy-start.84 = (f32[12,32]{1,0:T(8,128)S(1)}, f32[12,32]{1,0:T(8,128)}, u32[]{:S(2)}) copy-start(f32[12,32]{1,0:T(8,128)} %get-tuple-element.367) | copy-start | bytes 4612
  (141 other events, 996.6 us)
Sparse Core Ops, SparseCore 0:
  9.6 26.8 all-gather.12
  38.0 24.0 all-gather.22
  63.7 17.4 all-gather.18
  83.2 19.6 all-gather.16
  104.9 19.6 all-gather.14
  126.0 17.4 all-gather.20
  145.1 17.4 all-gather.28
  164.7 19.8 all-gather.26
  186.7 19.8 all-gather.24
  208.0 17.4 all-gather.30
  227.1 37.4 all-gather.32
  266.0 37.4 all-gather.34
  4827.8 28.1 reduce-scatter.10
  4858.6 28.1 reduce-scatter.12
  4889.1 28.1 reduce-scatter.14
  4919.9 28.1 reduce-scatter.16
  4958.4 94.2 all-reduce.18
  5055.6 25.8 reduce-scatter.18
  5084.9 25.7 reduce-scatter.20
  5113.6 25.7 reduce-scatter.22
  5142.2 25.7 reduce-scatter.24
  5170.5 47.8 reduce-scatter.26
  5221.0 47.8 reduce-scatter.28
  5273.9 172.5 all-reduce.16
where the time goes:
time: 5480 us; the launch traced here: 5470 us
  local copies, waits for them, and re-layouts  4540 us (83%)
  waiting for transfers between devices  576 us (11%)
  matrix products  226 us (4%)
    gather x12, local copies, waits for them, and re-layouts, bucket_onehot(): labels = jnp.take(buckets, offsets)  4350 us
    psum x1, waiting for transfers between devices, shards(): lax.psum(self_shares[2].astype(jnp.bfloat16), 'rep').astype(jnp.float32)  127 us
  transfers between devices with their start and end apart: 24, of which 15 were waited for; matrix products, arithmetic and copies ran while one was open for 57% of the time, Pallas kernels for 0%

commit v1 on v0

v1 whole, which is shorter than its diff:
```python
import functools
import types

import jax
import jax.numpy as jnp
from jax import lax
from jax.experimental import pallas as pl
from jax.experimental.pallas import tpu as pltpu
from jax.sharding import PartitionSpec as P

H = 12
HD = 64
LANES = 2 * HD
EPSILON = 1e-06
MASKED = -1e30
F32 = jnp.float32
BF16 = jnp.bfloat16
VMEM_LIMIT = 56 * 2**20
FUSED_LIMIT = 62 * 2**20
AHEAD = 2
SLOTS = 4
MESH = pl.DeviceIdType.MESH


def dot(a, b):
    return lax.dot_general(a, b, (((1,), (0,)), ((), ())), preferred_element_type=F32)


def dot_nt(a, b):
    return lax.dot_general(a, b, (((1,), (1,)), ((), ())), preferred_element_type=F32)


def dot_tn(a, b):
    return lax.dot_general(a, b, (((0,), (0,)), ((), ())), preferred_element_type=F32)


def rms_scale(values):
    return lax.rsqrt(jnp.mean(values * values, axis=-1, keepdims=True) + EPSILON)


def rms_back(values, gain, grad):
    scale = rms_scale(values)
    scaled = gain * grad
    mean = jnp.mean(scaled * values, axis=-1, keepdims=True)
    d_values = scale * scaled - values * (scale * scale * scale) * mean
    d_gain = jnp.sum(grad * values * scale, axis=0, keepdims=True)
    return d_values, d_gain


def gelu_parts(x):
    c = 0.7978845608028654
    t = jnp.tanh(c * (x + 0.044715 * (x * x * x)))
    value = 0.5 * x * (1.0 + t)
    slope = 0.5 * (1.0 + t) + 0.5 * x * (1.0 - t * t) * (c * (1.0 + 3.0 * 0.044715 * (x * x)))
    return value, slope


def own_lanes(first):
    lane = lax.broadcasted_iota(jnp.int32, (1, LANES), 1)
    mine = (lane < HD) if first else (lane >= HD)
    return jnp.where(mine, 1.0, 0.0)


def stack_heads(pair):
    one, two = own_lanes(True).astype(pair.dtype), own_lanes(False).astype(pair.dtype)
    return jnp.concatenate([pair * one, pair * two], axis=0)


def merge_heads(stacked):
    rows = stacked.shape[0] // 2
    return stacked[:rows] * own_lanes(True) + stacked[rows:] * own_lanes(False)


def skew(window, width):
    sub = lax.broadcasted_iota(jnp.int32, (8, width), 0)
    rows = jnp.broadcast_to(window, (8, width))
    for bit in (1, 2, 4):
        rows = jnp.where((sub & bit) != 0, pltpu.roll(rows, bit, 1), rows)
    return jnp.concatenate(
        [pltpu.roll(rows, (8 * g + width - 128) % width, 1) for g in range(16)], axis=0
    )


def unskew(total, width):
    sub = lax.broadcasted_iota(jnp.int32, (8, width), 0)
    rows = jnp.zeros((8, width), F32)
    for g in range(16):
        rows = rows + pltpu.roll(total[8 * g : 8 * g + 8], 128 - 8 * g, 1)
    for bit in (1, 2, 4):
        rows = jnp.where((sub & bit) != 0, pltpu.roll(rows, width - bit, 1), rows)
    return jnp.sum(rows, axis=0, keepdims=True)


def attend_kernel(biased, q_ref, k_ref, v_ref, *refs):
    if biased:
        row_ids, key_ids, window_ref, out_ref, p_ref = refs
    else:
        out_ref, p_ref = refs
    rows, length = q_ref.shape[0], k_ref.shape[0]
    blocks = rows // 128
    scores = dot_nt(stack_heads(q_ref[...]), k_ref[...])
    for head in range(2):
        if biased:
            width = window_ref.shape[2]
            table = skew(window_ref[0, head : head + 1, :], width)
        for b in range(blocks):
            at = head * rows + b * 128
            part = scores[at : at + 128]
            if biased:
                shift = (blocks - 1 - b) * 128
                allowed = key_ids[...] <= row_ids[b * 128 : b * 128 + 128, :]
                part = jnp.where(allowed, part + table[:, shift : shift + length], MASKED)
            top = jnp.max(part, axis=-1, keepdims=True)
            raised = jnp.exp(part - top)
            share = 1.0 / jnp.sum(raised, axis=-1, keepdims=True)
            p_ref[0, at : at + 128, :] = (raised * share).astype(BF16)
    out_ref[...] = merge_heads(dot(p_ref[0], v_ref[...]))


def attend_back_kernel(folded, q_ref, k_ref, v_ref, p_ref, out_ref, grad_ref, *refs):
    if folded:
        dq_ref, dk_ref, dv_ref, window_ref, ds_ref = refs
    else:
        dq_ref, dk_ref, dv_ref, ds_ref = refs
    rows, length = q_ref.shape[0], k_ref.shape[0]
    blocks = rows // 128
    grad = grad_ref[...]
    grads = stack_heads(grad)
    delta_wide = grad.astype(F32) * out_ref[...]
    d_weights = dot_nt(grads, v_ref[...])
    for head in range(2):
        if folded:
            width = window_ref.shape[2]
            total = jnp.zeros((128, width), F32)
        delta = jnp.sum(delta_wide * own_lanes(head == 0), axis=-1, keepdims=True)
        for b in range(blocks):
            at = head * rows + b * 128
            part = p_ref[0, at : at + 128, :].astype(F32) * (
                d_weights[at : at + 128] - delta[b * 128 : b * 128 + 128]
            )
            ds_ref[at : at + 128, :] = part.astype(BF16)
            if folded:
                shift = (blocks - 1 - b) * 128
                pieces = [part]
                if shift:
                    pieces = [jnp.zeros((128, shift), F32)] + pieces
                if width - shift - length:
                    pieces = pieces + [jnp.zeros((128, width - shift - length), F32)]
                total = total + jnp.concatenate(pieces, axis=1)
        if folded:
            window_ref[0, head : head + 1, :] = unskew(total, width)
    queries = stack_heads(q_ref[...])
    dq_ref[...] = merge_heads(dot(ds_ref[...], k_ref[...])).astype(BF16)
    dk_ref[...] = dot(queries.T, ds_ref[...]).T.astype(BF16)
    dv_ref[...] = dot(grads.T, p_ref[0]).T.astype(BF16)


def attend(query, keys, values, bias=None):
    rows, width = query.shape
    length = keys.shape[0]
    pairs = width // LANES
    column = lambda n: pl.BlockSpec((n, LANES), lambda i: (0, i))
    whole = lambda a: pl.BlockSpec(a.shape, lambda i: (0,) * a.ndim)
    operands, specs = [query, keys, values], [column(rows), column(length), column(length)]
    if bias is not None:
        row_ids, key_ids, window = bias
        operands += [row_ids, key_ids, window]
        specs += [
            whole(row_ids),
            whole(key_ids),
            pl.BlockSpec((1,) + window.shape[1:], lambda i: (i, 0, 0)),
        ]
    return pl.pallas_call(
        functools.partial(attend_kernel, bias is not None),
        grid=(pairs,),
        in_specs=specs,
        out_specs=[
            column(rows),
            pl.BlockSpec((1, 2 * rows, length), lambda i: (i, 0, 0)),
        ],
        out_shape=[
            jax.ShapeDtypeStruct((rows, width), F32),
            jax.ShapeDtypeStruct((pairs, 2 * rows, length), BF16),
        ],
        compiler_params=pltpu.CompilerParams(vmem_limit_bytes=VMEM_LIMIT),
        cost_estimate=pl.CostEstimate(
            flops=16 * rows * length * width,
            bytes_accessed=2 * pairs * 2 * rows * length,
            transcendentals=pairs * 2 * rows * length,
        ),
    )(*operands)


def attend_back(query, keys, values, weights, output, grad, window_shape=None):
    rows, width = query.shape
    length = keys.shape[0]
    pairs = width // LANES
    column = lambda n: pl.BlockSpec((n, LANES), lambda i: (0, i))
    out_specs = [column(rows), column(length), column(length)]
    out_shape = [
        jax.ShapeDtypeStruct((rows, width), BF16),
        jax.ShapeDtypeStruct((length, width), BF16),
        jax.ShapeDtypeStruct((length, width), BF16),
    ]
    if window_shape is not None:
        out_specs.append(pl.BlockSpec((1,) + window_shape[1:], lambda i: (i, 0, 0)))
        out_shape.append(jax.ShapeDtypeStruct(window_shape, F32))
    return pl.pallas_call(
        functools.partial(attend_back_kernel, window_shape is not None),
        grid=(pairs,),
        in_specs=[
            column(rows),
            column(length),
            column(length),
            pl.BlockSpec((1, 2 * rows, length), lambda i: (i, 0, 0)),
            column(rows),
            column(rows),
        ],
        out_specs=out_specs,
        out_shape=out_shape,
        scratch_shapes=[pltpu.VMEM((2 * rows, length), BF16)],
        compiler_params=pltpu.CompilerParams(vmem_limit_bytes=VMEM_LIMIT),
        cost_estimate=pl.CostEstimate(
            flops=32 * rows * length * width,
            bytes_accessed=2 * pairs * 2 * rows * length,
            transcendentals=0,
        ),
    )(query, keys, values, weights, output, grad)


def gather(values, axis=0):
    return lax.all_gather(values, "shard", axis=axis, tiled=True)


def scatter(values, axis=0):
    return lax.psum_scatter(values.astype(BF16), "shard", scatter_dimension=axis, tiled=True)


class Place:
    def __init__(self, reps, shards):
        self.nx, self.nz = shards // 2, reps // 2
        rep, shard = lax.axis_index("rep"), lax.axis_index("shard")
        self.rep, self.shard = rep, shard
        self.core, self.x = lax.rem(shard, 2), lax.div(shard, 2)
        self.y, self.z = lax.rem(rep, 2), lax.div(rep, 2)

    def other_core(self):
        return (self.rep, self.x * 2 + 1 - self.core)

    def x_at(self, step):
        x = lax.rem(self.x + step, self.nx)
        return x, (self.rep, x * 2 + self.core)

    def other_y(self):
        return (self.z * 2 + 1 - self.y, self.shard)

    def z_at(self, step):
        z = lax.rem(self.z + step, self.nz)
        return z, (z * 2 + self.y, self.shard)

    def partners(self):
        found = [self.other_core(), self.other_y()]
        found += [self.x_at(d)[1] for d in range(1, self.nx)]
        found += [self.z_at(d)[1] for d in range(1, self.nz)]
        return found


def enter(place):
    barrier = pltpu.get_barrier_semaphore()
    partners = place.partners()
    for device in partners:
        pl.semaphore_signal(barrier, inc=1, device_id=device, device_id_type=MESH)
    pl.semaphore_wait(barrier, len(partners))


def remote(src, dst, send, recv, device):
    return pltpu.make_async_remote_copy(
        src_ref=src, dst_ref=dst, send_sem=send, recv_sem=recv, device_id=device, device_id_type=MESH
    )


def added(*parts):
    total = parts[0].astype(F32)
    for part in parts[1:]:
        total = total + part.astype(F32)
    return total


class Reduction:
    def __init__(self, place, recv_a, recv_b, recv_c, recv_d, fin, send, recv, own_sem):
        self.place, self.recv_a, self.recv_b = place, recv_a, recv_b
        self.recv_c, self.recv_d, self.fin = recv_c, recv_d, fin
        self.send, self.recv, self.own_sem = send, recv, own_sem
        self.rows = recv_c.shape[1] // place.nz

    @staticmethod
    def scratch(n, nx, nz, q, half):
        copies = 3 + (nx - 1) + 2 * (nz - 1)
        return [
            pltpu.VMEM((n, nx, 2, q, half), BF16),
            pltpu.VMEM((n, nx - 1, 2, q, half), BF16),
            pltpu.VMEM((n, q, half), BF16),
            pltpu.VMEM((n, nz - 1, q // nz, half), BF16),
            pltpu.SemaphoreType.DMA((n, copies)),
            pltpu.SemaphoreType.DMA((n, copies)),
            pltpu.SemaphoreType.DMA((n,)),
        ]

    def copy(self, u, which, src, dst, device):
        return remote(src, dst, self.send.at[u, which], self.recv.at[u, which], device)

    def copies_a(self, u, src):
        return [self.copy(u, 0, src, self.recv_a.at[u], self.place.other_core())]

    def copies_b(self, u):
        p = self.place
        out = []
        for d in range(1, p.nx):
            x, device = p.x_at(d)
            out.append(self.copy(u, 2 + d, self.recv_a.at[u, x], self.recv_b.at[u, d - 1], device))
        return out

    def copies_c(self, u):
        p = self.place
        return [self.copy(u, 1, self.recv_b.at[u, 0, 1 - p.y], self.recv_c.at[u], p.other_y())]

    def copies_d(self, u):
        p, out = self.place, []
        for d in range(1, p.nz):
            z, device = p.z_at(d)
            src = self.recv_c.at[u, pl.ds(pl.multiple_of(z * self.rows, self.rows), self.rows)]
            out.append(self.copy(u, 1 + p.nx + d, src, self.recv_d.at[u, d - 1], device))
        return out

    def piece(self, u):
        p = self.place
        rows = pl.ds(pl.multiple_of(p.z * self.rows, self.rows), self.rows)
        return self.recv_c.at[u, rows], self.fin.at[u, p.y, rows]

    def copies_e(self, u):
        p, out = self.place, []
        for d in range(1, p.nz):
            out.append(self.copy(u, p.nx + p.nz + d, *self.piece(u), p.z_at(d)[1]))
        return out

    def keep(self, u):
        return pltpu.make_async_copy(*self.piece(u), self.own_sem.at[u])

    def copies_f(self, u):
        p = self.place
        return [self.copy(u, 2, self.fin.at[u, p.y], self.fin.at[u, p.y], p.other_y())]

    def start(self, copies):
        for copy in copies:
            copy.start()

    def arrived(self, copies):
        for copy in copies:
            copy.wait_recv()

    def begin(self, u, src):
        self.start(self.copies_a(u, src))

    def collect(self, u, src, own):
        self.arrived(self.copies_a(u, src))
        self.recv_a[u] = added(self.recv_a[u], own[...]).astype(BF16)

    def step_c(self, u):
        p = self.place
        self.arrived(self.copies_b(u))
        parts = [self.recv_a[u, p.x]] + [self.recv_b[u, d] for d in range(p.nx - 1)]
        self.recv_b[u, 0] = added(*parts).astype(BF16)
        self.start(self.copies_c(u))

    def step_d(self, u):
        self.arrived(self.copies_c(u))
        self.recv_c[u] = added(self.recv_b[u, 0, self.place.y], self.recv_c[u]).astype(BF16)
        self.start(self.copies_d(u))

    def step_e(self, u):
        p = self.place
        self.arrived(self.copies_d(u))
        rows = pl.ds(pl.multiple_of(p.z * self.rows, self.rows), self.rows)
        parts = [self.recv_c[u, rows]] + [self.recv_d[u, d] for d in range(p.nz - 1)]
        self.recv_c[u, rows] = added(*parts).astype(BF16)
        self.start(self.copies_e(u))
        self.keep(u).start()

    def step_f(self, u):
        self.arrived(self.copies_e(u))
        self.keep(u).wait()
        self.start(self.copies_f(u))

    def step_g(self, u):
        self.arrived(self.copies_f(u))

    def sent_rest(self, u):
        for copies in (self.copies_b(u), self.copies_c(u), self.copies_d(u), self.copies_e(u), self.copies_f(u)):
            for copy in copies:
                copy.wait_send()


class SmallSum:
    def __init__(self, place, held, landed, send, recv):
        self.place, self.held, self.landed = place, held, landed
        self.send, self.recv = send, recv

    @staticmethod
    def scratch(nx, nz, shape):
        copies = 2 + nx - 1 + nz - 1
        return [
            pltpu.VMEM((5,) + shape, F32),
            pltpu.VMEM((copies,) + shape, F32),
            pltpu.SemaphoreType.DMA((copies,)),
            pltpu.SemaphoreType.DMA((copies,)),
        ]

    def copies(self, stage):
        p = self.place
        first, devices = {
            0: (0, [p.other_core()]),
            1: (2, [p.x_at(d)[1] for d in range(1, p.nx)]),
            2: (1, [p.other_y()]),
            3: (1 + p.nx, [p.z_at(d)[1] for d in range(1, p.nz)]),
        }[stage]
        return [
            remote(self.held.at[stage], self.landed.at[first + i], self.send.at[first + i], self.recv.at[first + i], device)
            for i, device in enumerate(devices)
        ], list(range(first, first + len(devices)))

    def begin(self, value):
        self.held[0] = value
        self.launch()

    def launch(self):
        for copy in self.copies(0)[0]:
            copy.start()

    def step(self, stage, stages=4):
        copies, slots = self.copies(stage)
        for copy in copies:
            copy.wait_recv()
        total = self.held[stage]
        for slot in slots:
            total = total + self.landed[slot]
        self.held[stage + 1] = total
        if stage + 1 < stages:
            for copy in self.copies(stage + 1)[0]:
                copy.start()
        return total

    def sent(self, stages=4):
        for stage in range(stages):
            for copy in self.copies(stage)[0]:
                copy.wait_send()


class Gather:
    def __init__(self, place, whole, own, hidden_rows, send, recv, own_sem):
        self.place, self.whole, self.own = place, whole, own
        self.send, self.recv, self.own_sem = send, recv, own_sem
        self.width = whole.shape[1]
        self.q = self.width // (2 * place.nx)
        self.square = len(own) - hidden_rows // self.q
        self.hidden_rows = hidden_rows

    @staticmethod
    def scratch(units, nx):
        copies = 1 + 4 * (nx - 1)
        return [
            pltpu.SemaphoreType.DMA((units, copies)),
            pltpu.SemaphoreType.DMA((units, copies)),
            pltpu.SemaphoreType.DMA((units,)),
        ]

    def rows(self, u, shard, half=None):
        if isinstance(u, int) and u >= self.square:
            at = self.square * self.width + shard * self.hidden_rows + (u - self.square) * self.q
        else:
            at = u * self.width + shard * self.q
        if half is None:
            return pl.ds(pl.multiple_of(at, 16), self.q)
        return pl.ds(pl.multiple_of(at + half * (self.q // 2), 16), self.q // 2)

    def part(self, u, shard, half=None):
        return self.whole.at[self.rows(u, shard, half)]

    def copy(self, u, which, src, dst, device):
        return remote(src, dst, self.send.at[u, which], self.recv.at[u, which], device)

    def to_core(self, u):
        shard = self.place.shard
        return self.copy(u, 0, self.own[u], self.part(u, shard), self.place.other_core())

    def keep(self, u):
        return pltpu.make_async_copy(
            self.own[u], self.part(u, self.place.shard), self.own_sem.at[u]
        )

    def over_x(self, u, d):
        p = self.place
        half = self.own[u].at[pl.ds(pl.multiple_of(p.y * (self.q // 2), 16), self.q // 2)]
        return self.copy(u, 4 * d - 3, half, self.part(u, p.shard, p.y), p.x_at(d)[1])

    def came(self, d):
        p = self.place
        return lax.rem(p.x + p.nx - d, p.nx) * 2 + p.core

    def on_y(self, u, d):
        p = self.place
        here = self.part(u, self.came(d), p.y)
        return self.copy(u, 4 * d - 2, here, here, p.other_y())

    def on_core(self, u, d):
        p = self.place
        here = self.part(u, self.came(d), p.y)
        return self.copy(u, 4 * d - 1, here, here, p.other_core())

    def last_core(self, u, d):
        p = self.place
        here = self.part(u, self.came(d), 1 - p.y)
        return self.copy(u, 4 * d, here, here, p.other_core())

    def issue(self, u):
        for d in range(1, self.place.nx):
            self.over_x(u, d).start()
        self.to_core(u).start()
        self.keep(u).start()

    def relay_x(self, u):
        for d in range(1, self.place.nx):
            self.arrive_x(u, d)
            self.on_y(u, d).start()
            self.on_core(u, d).start()

    def arrive_x(self, u, d):
        p = self.place
        here = self.part(u, self.came(d), p.y)
        self.copy(u, 4 * d - 3, here, here, p.x_at(d)[1]).wait_recv()

    def relay_y(self, u):
        for d in range(1, self.place.nx):
            self.on_y(u, d).wait_recv()
            self.last_core(u, d).start()

    def ready(self, u):
        p = self.place
        here = self.part(u, p.shard)
        pltpu.make_async_copy(here, here, self.own_sem.at[u]).wait()
        self.copy(u, 0, here, here, p.other_core()).wait_recv()
        for d in range(1, p.nx):
            self.on_core(u, d).wait_recv()
            self.last_core(u, d).wait_recv()

    def sent(self, u):
        p = self.place
        here = self.part(u, p.shard)
        self.copy(u, 0, here, here, p.other_core()).wait_send()
        for d in range(1, p.nx):
            here = self.part(u, self.came(d), p.y)
            self.copy(u, 4 * d - 3, here, here, p.x_at(d)[1]).wait_send()
            self.on_y(u, d).wait_send()
            self.on_core(u, d).wait_send()
            self.last_core(u, d).wait_send()


class Spread:
    def __init__(self, place, own, whole, send, recv, own_sem):
        self.place, self.own, self.whole = place, own, whole
        self.send, self.recv, self.own_sem = send, recv, own_sem
        self.count = own.shape[0]

    @staticmethod
    def scratch(nx):
        copies = 1 + 2 * (nx - 1)
        return [
            pltpu.SemaphoreType.DMA((copies,)),
            pltpu.SemaphoreType.DMA((copies,)),
            pltpu.SemaphoreType.DMA(()),
        ]

    def part(self, shard):
        return self.whole.at[pl.ds(pl.multiple_of(shard * self.count, 16), self.count)]

    def copy(self, which, src, dst, device):
        return remote(src, dst, self.send.at[which], self.recv.at[which], device)

    def to_core(self):
        return self.copy(0, self.own, self.part(self.place.shard), self.place.other_core())

    def over_x(self, d):
        p = self.place
        return self.copy(2 * d - 1, self.own, self.part(p.shard), p.x_at(d)[1])

    def on_core(self, d):
        p = self.place
        here = self.part(lax.rem(p.x + p.nx - d, p.nx) * 2 + p.core)
        return self.copy(2 * d, here, here, p.other_core())

    def keep(self):
        return pltpu.make_async_copy(self.own, self.part(self.place.shard), self.own_sem)

    def issue(self):
        for d in range(1, self.place.nx):
            self.over_x(d).start()
        self.to_core().start()
        self.keep().start()

    def relay_x(self):
        for d in range(1, self.place.nx):
            self.over_x(d).wait_recv()
            self.on_core(d).start()

    def ready(self):
        self.keep().wait()
        self.to_core().wait_recv()
        for d in range(1, self.place.nx):
            self.on_core(d).wait_recv()

    def sent(self):
        self.to_core().wait_send()
        for d in range(1, self.place.nx):
            self.over_x(d).wait_send()
            self.on_core(d).wait_send()


def attend_pair(query, keys, values_ref, p_ref, bias=None):
    rows, length = query.shape[0], keys.shape[0]
    blocks = rows // 128
    scores = dot_nt(stack_heads(query), keys)
    for head in range(2):
        if bias is not None:
            row_ids, key_ids, window = bias
            table = skew(window[head : head + 1], window.shape[1])
        for b in range(blocks):
            at = head * rows + b * 128
            part = scores[at : at + 128]
            if bias is not None:
                shift = (blocks - 1 - b) * 128
                allowed = key_ids <= row_ids[b * 128 : b * 128 + 128]
                part = jnp.where(allowed, part + table[:, shift : shift + length], MASKED)
            top = jnp.max(part, axis=-1, keepdims=True)
            raised = jnp.exp(part - top)
            share = 1.0 / jnp.sum(raised, axis=-1, keepdims=True)
            p_ref[at : at + 128, :] = (raised * share).astype(BF16)
    return merge_heads(dot(p_ref[...], values_ref[...]))


def forward_kernel(reps, shards, names, *refs):
    r = types.SimpleNamespace(**dict(zip(names, refs)))
    place = Place(reps, shards)
    rows, width = r.tok_in.shape
    length = r.tok.shape[0]
    pairs = width // LANES
    q = width // shards
    part = r.feed_in.shape[1] // width
    own = [r.self_query, r.self_keyval.at[0], r.self_keyval.at[1], r.self_output]
    own += [r.cross_query, r.cross_keyval.at[0], r.cross_keyval.at[1], r.cross_output]
    own += [r.feed_in.at[:, pl.ds(j * width, width)] for j in range(part)]
    own += [r.feed_out.at[pl.ds(j * q, q)] for j in range(part)]
    units = len(own)
    small = SmallSum(place, r.small_held, r.small_landed, r.small_send, r.small_recv)
    gather = Gather(place, r.whole, own, r.feed_out.shape[0], r.w_send, r.w_recv, r.w_own)
    tokens = Spread(place, r.tok_in, r.tok, r.t_send, r.t_recv, r.t_own)
    memories = Spread(place, r.enc_in, r.enc, r.e_send, r.e_recv, r.e_own)

    def weight(u):
        return r.whole[pl.ds(pl.multiple_of(u * width, width), width), :]

    def emit_weights(u, count):
        block = pl.ds(u * width, count * width)
        return pltpu.make_async_copy(r.whole.at[block], r.w_out.at[block], r.out_sem.at[u])

    def emit_kv(i):
        return pltpu.make_async_copy(r.kv.at[i], r.kv_out.at[i], r.out_sem.at[units + i])

    emit_tok = pltpu.make_async_copy(r.tok_t, r.tok_out, r.out_sem.at[units + 4])
    emit_enc = pltpu.make_async_copy(r.enc_t, r.enc_out, r.out_sem.at[units + 5])

    def emit_p(which, i):
        slot = lax.rem(i, 2)
        return pltpu.make_async_copy(r.probs.at[slot], r.p_out.at[which, i], r.p_sem.at[slot])

    def gain(i):
        return r.small_held[2, i : i + 1, :width]

    enter(place)
    small.begin(r.small_in[...])
    line = [(gather, (u,)) for u in (1, 2, 0)] + [(tokens, ()), (memories, ())]
    line += [(gather, (u,)) for u in [3, 5, 6, 4, 7] + list(range(8, units))]

    def issue(at):
        if at < len(line):
            line[at][0].issue(*line[at][1])

    def relay(owner, *u):
        owner.relay_x(*u)
        issue(line.index((owner, u)) + AHEAD)

    for at in range(AHEAD):
        issue(at)
    small.step(0, 2)
    gathered = small.step(1, 2)
    r.small_out[...] = gathered
    table = gathered[8:24, :LANES].astype(BF16)
    biases = dot(table, r.onehot[...])
    for i in range(pairs):
        r.window[i] = biases[2 * i : 2 * i + 2]
    for u in (1, 2, 0):
        relay(gather, u)
    for u in (1, 2, 0):
        gather.relay_y(u)
    relay(tokens)
    tokens.ready()
    tokens.sent()

    def norm_rows(i, carry):
        at = pl.ds(pl.multiple_of(i * rows, 16), rows)
        values = r.tok[at, :].astype(F32)
        normed = (values * rms_scale(values) * gain(0)).astype(BF16)
        r.tok[at, :] = normed
        r.tok_t[:, pl.ds(pl.multiple_of(i * rows, LANES), rows)] = normed.T
        return carry

    lax.fori_loop(0, length // rows, norm_rows, 0)
    emit_tok.start()

    def project_pair(source, target, base):
        def step(i, carry):
            at = pl.ds(pl.multiple_of(i * rows, 16), rows)
            block = source[at, :]
            for which in range(2):
                out = dot(block, weight(base + which)).astype(BF16)
                for j in range(pairs):
                    r.kv[target + which, j, at, :] = out[:, j * LANES : (j + 1) * LANES]
            return carry

        lax.fori_loop(0, source.shape[0] // rows, step, 0)
        emit_kv(target).start()
        emit_kv(target + 1).start()

    def project_query(normed, u, which):
        out = dot(normed, weight(u)).astype(BF16)
        for j in range(pairs):
            r.q_out[which, j] = out[:, j * LANES : (j + 1) * LANES]

    def attention(which, bias, relays):
        def pair(i, carry):
            @pl.when(i >= 2)
            def _():
                emit_p(which, i).wait()

            slot = lax.rem(i, 2)
            more = None
            if bias:
                more = (r.row_ids[...], r.small_held[2, 3:4, :length], r.window[i])
            r.low_out[which, i] = attend_pair(
                r.q_out[which, i],
                r.kv[2 * which, i],
                r.kv.at[2 * which + 1, i],
                r.probs.at[slot],
                more,
            )
            emit_p(which, i).start()
            for step, relay, u in relays:
                @pl.when(i == step)
                def _():
                    relay(*u)

            return carry

        lax.fori_loop(0, pairs, pair, 0)
        emit_p(which, 0).wait()
        emit_p(which, 1).wait()
        low = [r.low_out[which, j].astype(BF16) for j in range(pairs)]
        low = jnp.concatenate(low, axis=1)
        r.low_t[which] = low.T
        return low

    gather.ready(1)
    gather.ready(2)
    project_pair(r.tok, 0, 1)
    gather.ready(0)
    emit_weights(0, 3).start()
    mine = pl.ds(pl.multiple_of(place.shard * rows, 16), rows)
    project_query(r.tok[mine, :], 0, 0)
    over_y = gather.relay_y

    def over_x(u):
        relay(gather, u)

    low = attention(
        0,
        True,
        [
            (0, relay, (memories,)),
            (1, over_x, (3,)),
            (2, over_x, (5,)),
            (3, over_x, (6,)),
            (3, over_y, (3,)),
            (4, over_x, (4,)),
            (4, over_y, (5,)),
            (5, over_y, (6,)),
        ],
    )
    gather.ready(3)
    r.first_out[...] = r.tok_in[...].astype(F32) + dot(low, weight(3))
    over_x(7)
    over_y(4)
    memories.ready()

    def turn_rows(i, carry):
        at = pl.ds(pl.multiple_of(i * rows, LANES), rows)
        r.enc_t[:, at] = r.enc[at, :].T
        return carry

    lax.fori_loop(0, length // rows, turn_rows, 0)
    emit_enc.start()
    gather.ready(5)
    gather.ready(6)
    project_pair(r.enc, 2, 5)
    gather.ready(4)
    first = r.first_out[...]
    normed = (first * rms_scale(first) * gain(1)).astype(BF16)
    r.normed2_t[...] = normed.T
    project_query(normed, 4, 1)
    over_x(8)
    over_y(7)
    low = attention(
        1,
        False,
        [
            (1, over_x, (9,)),
            (1, over_y, (8,)),
            (2, over_x, (10,)),
            (3, over_y, (9,)),
            (4, over_x, (11,)),
            (5, over_y, (10,)),
        ],
    )
    gather.ready(7)
    emit_weights(3, 5).start()
    r.second_out[...] = r.first_out[...] + dot(low, weight(7))
    over_x(12)
    over_y(11)
    second = r.second_out[...]
    normed = (second * rms_scale(second) * gain(2)).astype(BF16)
    r.normed[...] = normed
    r.normed3_t[...] = normed.T
    for j in range(part):
        gather.ready(8 + j)
        value, slope = gelu_parts(dot(r.normed[...], weight(8 + j)))
        value = value.astype(BF16)
        r.hidden[j] = value
        r.hidden_t[j * width : (j + 1) * width, :] = value.T
        r.slope_out[j] = slope
        if j + 1 < part:
            over_x(13 + j)
            over_y(12 + j)
    over_y(units - 1)
    for j in range(part):
        gather.ready(8 + part + j)
    emit_weights(8, units - 8).start()
    total = second
    for j in range(part):
        total = total + dot(r.hidden[j], weight(8 + part + j))
    r.result[...] = total.astype(BF16)
    for u in range(units):
        gather.sent(u)
    memories.sent()
    small.sent(2)
    for u, count in ((0, 3), (3, 5), (8, units - 8)):
        emit_weights(u, count).wait()
    for i in range(4):
        emit_kv(i).wait()
    emit_tok.wait()
    emit_enc.wait()


def forward(tokens, encoded, row_ids, small, onehot, shards_of, reps, shards):
    rows, width = tokens.shape
    length, memory = rows * shards, encoded.shape[0] * shards
    nx = shards // 2
    feed_in, feed_out = shards_of[-2:]
    hidden = feed_in.shape[1]
    units = 8 + 2 * (hidden // width)
    pairs = width // LANES
    kept = lambda *shape, dtype=BF16: (pl.BlockSpec(memory_space=pl.ANY), jax.ShapeDtypeStruct(shape, dtype))
    near = lambda *shape, dtype=F32: (pl.BlockSpec(memory_space=pltpu.VMEM), jax.ShapeDtypeStruct(shape, dtype))
    outs = dict(
        result=near(rows, width, dtype=BF16),
        first_out=near(rows, width),
        second_out=near(rows, width),
        low_out=near(2, pairs, rows, LANES),
        q_out=near(2, pairs, rows, LANES, dtype=BF16),
        small_out=near(*small.shape),
        low_t=near(2, width, rows, dtype=BF16),
        normed2_t=near(width, rows, dtype=BF16),
        normed3_t=near(width, rows, dtype=BF16),
        hidden_t=near(hidden, rows, dtype=BF16),
        slope_out=near(hidden // width, rows, width),
        w_out=kept(units * width, width),
        kv_out=kept(4, pairs, length, LANES),
        tok_out=kept(width, length),
        enc_out=kept(width, memory),
        p_out=kept(2, pairs, 2 * rows, length),
    )
    scratch = dict(
        whole=pltpu.VMEM((units * width, width), BF16),
        tok=pltpu.VMEM((length, width), BF16),
        enc=pltpu.VMEM((memory, width), BF16),
        kv=pltpu.VMEM((4, pairs, length, LANES), BF16),
        window=pltpu.VMEM((pairs, 2, onehot.shape[1]), F32),
        probs=pltpu.VMEM((2, 2 * rows, length), BF16),
        normed=pltpu.VMEM((rows, width), BF16),
        hidden=pltpu.VMEM((hidden // width, rows, width), BF16),
        tok_t=pltpu.VMEM((width, length), BF16),
        enc_t=pltpu.VMEM((width, memory), BF16),
        p_sem=pltpu.SemaphoreType.DMA((2,)),
        out_sem=pltpu.SemaphoreType.DMA((units + 6,)),
    )
    scratch.update(zip(("small_held", "small_landed", "small_send", "small_recv"), SmallSum.scratch(nx, reps // 2, small.shape)))
    scratch.update(zip(("w_send", "w_recv", "w_own"), Gather.scratch(units, nx)))
    scratch.update(zip(("t_send", "t_recv", "t_own"), Spread.scratch(nx)))
    scratch.update(zip(("e_send", "e_recv", "e_own"), Spread.scratch(nx)))
    shard_names = ["self_query", "self_keyval", "self_output", "cross_query", "cross_keyval", "cross_output", "feed_in", "feed_out"]
    names = ["tok_in", "enc_in", "row_ids", "small_in", "onehot"] + shard_names + list(outs) + list(scratch)
    made = pl.pallas_call(
        functools.partial(forward_kernel, reps, shards, tuple(names)),
        in_specs=[pl.BlockSpec(memory_space=pltpu.VMEM)] * 5 + [pl.BlockSpec(memory_space=pl.ANY)] * 8,
        out_specs=[spec for spec, _ in outs.values()],
        out_shape=[shape for _, shape in outs.values()],
        scratch_shapes=list(scratch.values()),
        compiler_params=pltpu.CompilerParams(
            collective_id=2, has_side_effects=True, vmem_limit_bytes=FUSED_LIMIT
        ),
    )(tokens, encoded, row_ids, small, onehot, *shards_of)
    return types.SimpleNamespace(**dict(zip(outs, made)))


class RowSum:
    def __init__(self, place, parts, recv_a, recv_b, send, recv):
        self.place, self.parts, self.recv_a, self.recv_b = place, parts, recv_a, recv_b
        self.send, self.recv = send, recv

    @staticmethod
    def scratch(nx, width, rows):
        return [
            pltpu.VMEM((2, nx, width, rows), BF16),
            pltpu.VMEM((nx, width, rows), BF16),
            pltpu.VMEM((nx - 1, width, rows), BF16),
            pltpu.SemaphoreType.DMA((nx,)),
            pltpu.SemaphoreType.DMA((nx,)),
        ]

    def copy(self, which, src, dst, device):
        return remote(src, dst, self.send.at[which], self.recv.at[which], device)

    def to_core(self):
        p = self.place
        return self.copy(0, self.parts.at[1 - p.core], self.recv_a, p.other_core())

    def over_x(self, d):
        x, device = self.place.x_at(d)
        return self.copy(d, self.recv_a.at[x], self.recv_b.at[d - 1], device)

    def begin(self, total):
        rows = self.parts.shape[3]
        for s in range(2 * self.place.nx):
            self.parts[s % 2, s // 2] = total[:, s * rows : (s + 1) * rows].astype(BF16)
        self.to_core().start()

    def pass_x(self):
        self.to_core().wait_recv()
        self.recv_a[...] = added(self.recv_a[...], self.parts[self.place.core]).astype(BF16)
        for d in range(1, self.place.nx):
            self.over_x(d).start()

    def finish(self):
        p = self.place
        for d in range(1, p.nx):
            self.over_x(d).wait_recv()
        return added(self.recv_a[p.x], *[self.recv_b[d] for d in range(p.nx - 1)])

    def sent(self):
        for d in range(1, self.place.nx):
            self.over_x(d).wait_send()


def attend_back_pair(query, keys, values, p_ref, output, grad, ds_ref, width=None):
    rows, length = query.shape[0], keys.shape[0]
    blocks = rows // 128
    grads, queries = stack_heads(grad), stack_heads(query)
    delta_wide = grad.astype(F32) * output
    d_weights = dot_nt(grads, values)
    windows = []
    for head in range(2):
        delta = jnp.sum(delta_wide * own_lanes(head == 0), axis=-1, keepdims=True)
        total = None
        for b in range(blocks):
            at = head * rows + b * 128
            part = p_ref[at : at + 128, :].astype(F32) * (
                d_weights[at : at + 128] - delta[b * 128 : b * 128 + 128]
            )
            ds_ref[at : at + 128, :] = part.astype(BF16)
            if width is not None:
                shift = (blocks - 1 - b) * 128
                pieces = [jnp.zeros((128, shift), F32)] if shift else []
                pieces.append(part)
                if width - shift - length:
                    pieces.append(jnp.zeros((128, width - shift - length), F32))
                placed = jnp.concatenate(pieces, axis=1)
                total = placed if total is None else total + placed
        if width is not None:
            windows.append(unskew(total, width))
    d_query = merge_heads(dot(ds_ref[...], keys)).astype(BF16)
    d_keys = dot(queries.T, ds_ref[...]).astype(BF16)
    d_values = dot(grads.T, p_ref[...]).astype(BF16)
    return d_query, d_keys, d_values, windows


def backward_kernel(reps, shards, names, *refs):
    r = types.SimpleNamespace(**dict(zip(names, refs)))
    place = Place(reps, shards)
    rows, width = r.cotangent.shape
    length = r.enc_t.shape[1]
    pairs = width // LANES
    q = width // shards
    part = r.hidden_t.shape[0] // width
    units = 8 + 2 * part
    red = Reduction(place, r.recv_a, r.recv_b, r.recv_c, r.recv_d, r.fin, r.r_send, r.r_recv, r.r_own)
    small = SmallSum(place, r.small_held, r.small_landed, r.small_send, r.small_recv)
    sum_memory = RowSum(place, r.m_parts, r.m_a, r.m_b, r.m_send, r.m_recv)
    sum_tokens = RowSum(place, r.m_parts, r.t_a, r.t_b, r.t_send, r.t_recv)

    def gain(i):
        return r.gains[i : i + 1, :width]

    def load_weight(u, slot):
        block = pl.ds(u * width, width)
        return pltpu.make_async_copy(r.w_in.at[block], r.w.at[slot], r.w_sem.at[slot])

    def load_slope(j):
        slot = lax.rem(j, 2)
        return pltpu.make_async_copy(r.slope.at[j], r.slopes.at[slot], r.s_sem.at[slot])

    def load_kv(i, slot):
        return pltpu.make_async_copy(r.kv_in.at[i], r.kv.at[slot], r.kv_sem.at[slot])

    def load_p(which, i):
        slot = lax.rem(i, 2)
        return pltpu.make_async_copy(r.p_in.at[which, i], r.probs.at[slot], r.p_sem.at[slot])

    def load_t(source, which):
        return pltpu.make_async_copy(source, r.rows_t, r.t_sem.at[which])

    def away(n):
        return r.made.at[lax.rem(n, SLOTS), 1 - place.core]

    def fill(n, value):
        slot = lax.rem(n, SLOTS)
        rest = value.shape[0] // shards
        half = width // 2
        for s in range(shards):
            for h in range(2):
                r.made[slot, s % 2, s // 2, h] = value[
                    s * rest : (s + 1) * rest, h * half : (h + 1) * half
                ].astype(BF16)
        red.begin(n, away(n))

    def free(n):
        red.copies_a(n - SLOTS, away(n))[0].wait_send()

    def take(n):
        red.collect(n, away(n), r.made.at[lax.rem(n, SLOTS), place.core])

    def advance(n):
        if n < units:
            red.step_c(n)
            if n + AHEAD < units:
                red.start(red.copies_b(n + AHEAD))
        for late, step in ((1, red.step_d), (2, red.step_e), (3, red.step_f), (4, red.step_g)):
            if 0 <= n - late < units:
                step(n - late)

    enter(place)
    load_slope(0).start()
    for slot, u in enumerate((8, 8 + part)):
        load_weight(u, slot).start()
    for slot in range(2):
        load_kv(2 + slot, slot).start()
        load_p(1, slot).start()
    load_t(r.enc_t, 0).start()
    r.acc[...] = jnp.zeros((rows, width), F32)

    def feed(j, carry):
        slot = 2 * lax.rem(j, 2)
        load_weight(8, slot).wait()
        load_weight(8 + part, slot + 1).wait()
        load_slope(j).wait()

        @pl.when(j + 1 < part)
        def _():
            load_slope(j + 1).start()
            load_weight(8 + j + 1, 2 - slot).start()
            load_weight(8 + part + j + 1, 3 - slot).start()

        grad_hidden = dot_nt(r.cotangent[...], r.w[slot + 1])
        grad = (grad_hidden * r.slopes[lax.rem(j, 2)]).astype(BF16)
        fill(j, dot(r.normed3_t[...], grad))
        r.acc[...] += dot_nt(grad, r.w[slot])

        @pl.when(j >= 1)
        def _():
            take(j - 1)

        return carry

    lax.fori_loop(0, part, feed, 0)
    for slot, u in ((0, 7), (1, 5), (2, 6), (3, 4)):
        load_weight(u, slot).start()
    take(part - 1)
    for n in range(AHEAD):
        red.start(red.copies_b(n))

    def feed_out(m, carry):
        n = part + m
        free(n)
        value = jnp.concatenate(
            [
                dot(
                    r.hidden_t[pl.ds(pl.multiple_of(s * width + m * q, 16), q), :],
                    r.cotangent[...],
                )
                for s in range(shards)
            ],
            axis=0,
        )
        fill(n, value)

        @pl.when(m >= 1)
        def _():
            take(n - 1)

        return carry

    lax.fori_loop(0, part, feed_out, 0)
    back, d_gain3 = rms_back(r.second[...], gain(2), r.acc[...])
    r.grad[...] = r.cotangent[...].astype(F32) + back
    take(2 * part - 1)

    def attention(which, fold, steps):
        def pair(i, carry):
            slot = lax.rem(i, 2)
            load_p(which, i).wait()
            d_query, d_keys, d_values, windows = attend_back_pair(
                r.queries[which, i],
                r.kv[0, i],
                r.kv[1, i],
                r.probs.at[slot],
                r.low[which, i],
                r.grad_att[i],
                r.ds,
                r.onehot.shape[1] if fold else None,
            )
            r.d_query[i] = d_query
            at = pl.ds(pl.multiple_of(i * LANES, LANES), LANES)
            r.dk_t[at, :] = d_keys
            r.dv_t[at, :] = d_values
            if fold:
                r.d_window[i] = jnp.concatenate(windows, axis=0)

            @pl.when(i + 2 < pairs)
            def _():
                load_p(which, i + 2).start()

            for step, n in steps:
                @pl.when(i == step)
                def _():
                    advance(n)

            return carry

        lax.fori_loop(0, pairs, pair, 0)

    def spread_grad(value):
        for i in range(pairs):
            r.grad_att[i] = value[:, i * LANES : (i + 1) * LANES].astype(BF16)

    def joined_query():
        return jnp.concatenate([r.d_query[i] for i in range(pairs)], axis=1)

    n = 2 * part
    grad_low = r.grad[...].astype(BF16)
    free(n)
    fill(n, dot(r.low_t[1], grad_low))
    load_weight(7, 0).wait()
    spread_grad(dot_nt(grad_low, r.w[0]))
    load_weight(3, 0).start()
    take(n)
    for slot in range(2):
        load_kv(2 + slot, slot).wait()
    attention(1, False, [(0, 0), (4, 1)])
    for slot in range(2):
        load_kv(slot, slot).start()
        load_p(0, slot).start()
    load_weight(5, 1).wait()
    load_weight(6, 2).wait()
    sum_memory.begin(dot(r.w[1], r.dk_t[...]) + dot(r.w[2], r.dv_t[...]))
    load_weight(1, 1).start()
    load_weight(2, 2).start()
    load_t(r.enc_t, 0).wait()
    free(n + 1)
    fill(n + 1, dot_nt(r.rows_t[...], r.dk_t[...]))
    sum_memory.pass_x()
    free(n + 2)
    fill(n + 2, dot_nt(r.rows_t[...], r.dv_t[...]))
    take(n + 1)
    load_t(r.tok_t, 1).start()
    d_query = joined_query()
    load_weight(4, 3).wait()
    back, d_gain2 = rms_back(r.first[...], gain(1), dot_nt(d_query, r.w[3]))
    load_weight(0, 3).start()
    free(n + 3)
    fill(n + 3, dot(r.normed2_t[...], d_query))
    take(n + 2)
    r.grad[...] = r.grad[...] + back
    advance(2)

    grad_low = r.grad[...].astype(BF16)
    take(n + 3)
    free(n + 4)
    fill(n + 4, dot(r.low_t[0], grad_low))
    load_weight(3, 0).wait()
    spread_grad(dot_nt(grad_low, r.w[0]))
    take(n + 4)
    for slot in range(2):
        load_kv(slot, slot).wait()
    attention(0, True, [(1, 3), (4, 4)])
    load_weight(1, 1).wait()
    load_weight(2, 2).wait()
    sum_memory.to_core().wait_send()
    sum_tokens.begin(dot(r.w[1], r.dk_t[...]) + dot(r.w[2], r.dv_t[...]))
    load_t(r.tok_t, 1).wait()
    free(n + 5)
    fill(n + 5, dot_nt(r.rows_t[...], r.dk_t[...]))
    sum_tokens.pass_x()
    free(n + 6)
    fill(n + 6, dot_nt(r.rows_t[...], r.dv_t[...]))
    take(n + 5)
    r.d_memory[...] = sum_memory.finish().T
    advance(5)
    d_query = joined_query()
    free(n + 7)
    mine = pl.ds(pl.multiple_of(place.shard * rows, LANES), rows)
    fill(n + 7, dot(r.rows_t[:, mine], d_query))
    take(n + 6)
    load_weight(0, 3).wait()
    r.acc[...] = dot_nt(d_query, r.w[3])
    windows = jnp.concatenate([r.d_window[i] for i in range(pairs)], axis=0)
    d_table = lax.dot_general(
        windows,
        r.onehot[...].astype(F32),
        (((1,), (1,)), ((), ())),
        precision=lax.Precision.HIGHEST,
        preferred_element_type=F32,
    )
    take(n + 7)
    advance(6)
    values = r.tokens[...].astype(F32)
    back, d_gain1 = rms_back(values, gain(0), r.acc[...] + sum_tokens.finish().T)
    r.d_tokens[...] = r.grad[...] + back
    r.small_held[0] = jnp.zeros(r.small_held.shape[1:], F32)
    for i, d_gain in enumerate((d_gain1, d_gain2, d_gain3)):
        r.small_held[0, i : i + 1, :width] = d_gain
    r.small_held[0, 8 : 8 + 2 * pairs, :LANES] = d_table
    small.launch()
    for n in range(7, units + 4):
        advance(n)
        if n < 11:
            small.step(n - 7)
    r.small_out[...] = r.small_held[4]
    for n in range(units):
        if n >= units - SLOTS:
            red.copies_a(n, away(n))[0].wait_send()
        red.sent_rest(n)
    small.sent()
    sum_tokens.to_core().wait_send()
    sum_memory.sent()
    sum_tokens.sent()


def backward(tokens, cotangent, onehot, held, reps, shards):
    rows, width = tokens.shape
    length = held.enc_out.shape[1]
    nx, nz = shards // 2, reps // 2
    pairs = width // LANES
    q, half = width // shards, width // 2
    units = held.w_out.shape[0] // width
    small = (24, width)
    kept = pl.BlockSpec(memory_space=pl.ANY)
    near = pl.BlockSpec(memory_space=pltpu.VMEM)
    ins = dict(
        tokens=(near, tokens),
        cotangent=(near, cotangent),
        onehot=(near, onehot),
        gains=(near, held.small_out),
        first=(near, held.first_out),
        second=(near, held.second_out),
        low=(near, held.low_out),
        low_t=(near, held.low_t),
        queries=(near, held.q_out),
        normed2_t=(near, held.normed2_t),
        normed3_t=(near, held.normed3_t),
        hidden_t=(near, held.hidden_t),
        slope=(kept, held.slope_out),
        tok_t=(kept, held.tok_out),
        enc_t=(kept, held.enc_out),
        w_in=(kept, held.w_out),
        kv_in=(kept, held.kv_out),
        p_in=(kept, held.p_out),
    )
    outs = dict(
        d_tokens=(near, jax.ShapeDtypeStruct((rows, width), F32)),
        d_memory=(near, jax.ShapeDtypeStruct((rows, width), F32)),
        small_out=(near, jax.ShapeDtypeStruct(small, F32)),
        fin=(kept, jax.ShapeDtypeStruct((units, 2, q, half), BF16)),
    )
    scratch = dict(
        w=pltpu.VMEM((4, width, width), BF16),
        kv=pltpu.VMEM((2, pairs, length, LANES), BF16),
        probs=pltpu.VMEM((2, 2 * rows, length), BF16),
        ds=pltpu.VMEM((2 * rows, length), BF16),
        rows_t=pltpu.VMEM((width, length), BF16),
        dk_t=pltpu.VMEM((width, length), BF16),
        dv_t=pltpu.VMEM((width, length), BF16),
        d_query=pltpu.VMEM((pairs, rows, LANES), BF16),
        grad_att=pltpu.VMEM((pairs, rows, LANES), BF16),
        d_window=pltpu.VMEM((pairs, 2, onehot.shape[1]), F32),
        acc=pltpu.VMEM((rows, width), F32),
        grad=pltpu.VMEM((rows, width), F32),
        made=pltpu.VMEM((SLOTS, 2, nx, 2, q, half), BF16),
        slopes=pltpu.VMEM((2, rows, width), F32),
        s_sem=pltpu.SemaphoreType.DMA((2,)),
        w_sem=pltpu.SemaphoreType.DMA((4,)),
        kv_sem=pltpu.SemaphoreType.DMA((2,)),
        p_sem=pltpu.SemaphoreType.DMA((2,)),
        t_sem=pltpu.SemaphoreType.DMA((2,)),
    )
    scratch.update(
        zip(
            ("recv_a", "recv_b", "recv_c", "recv_d", "r_send", "r_recv", "r_own"),
            Reduction.scratch(units, nx, nz, q, half),
        )
    )
    scratch.update(
        zip(("small_held", "small_landed", "small_send", "small_recv"), SmallSum.scratch(nx, nz, small))
    )
    for name in "mt":
        keys = (name + end for end in ("_parts", "_a", "_b", "_send", "_recv"))
        scratch.update(zip(keys, RowSum.scratch(nx, width, rows)))
    del scratch["t_parts"]
    names = tuple(list(ins) + list(outs) + list(scratch))
    made = pl.pallas_call(
        functools.partial(backward_kernel, reps, shards, names),
        in_specs=[spec for spec, _ in ins.values()],
        out_specs=[spec for spec, _ in outs.values()],
        out_shape=[shape for _, shape in outs.values()],
        scratch_shapes=list(scratch.values()),
        compiler_params=pltpu.CompilerParams(
            collective_id=3, has_side_effects=True, vmem_limit_bytes=FUSED_LIMIT
        ),
    )(*[value for _, value in ins.values()])
    return types.SimpleNamespace(**dict(zip(outs, made)))


def tiles_evenly(reps, shards, width):
    if reps % 2 or shards % 2 or width % shards:
        return False
    return (width // shards) % (8 * reps) == 0 and width % (4 * HD) == 0


def layer(
    tokens,
    encoded,
    block_ids,
    buckets,
    cotangent,
    norm_self,
    self_query,
    self_keyval,
    self_output,
    bucket_bias,
    norm_cross,
    cross_query,
    cross_keyval,
    cross_output,
    norm_feed,
    feed_in,
    feed_out,
):
    groups, positions, model_width = tokens.shape
    reps, shards = lax.axis_size("rep"), lax.axis_size("shard")
    length = (buckets.shape[0] + 1) // 2
    memory_local = encoded.shape[1]
    row_anchor = lax.axis_index("shard") * positions
    heads, bucket_count = bucket_bias.shape[0], bucket_bias.shape[1] * shards
    window_width = length + positions
    window_buckets = lax.dynamic_slice_in_dim(
        jnp.pad(buckets, (1, 0)), length - row_anchor - positions, window_width
    )
    fused = tiles_evenly(reps, shards, model_width) and encoded.shape == tokens.shape
    fused = fused and feed_out.shape[0] == model_width and positions % LANES == 0
    if fused:
        onehot = window_buckets[None, :] == jnp.arange(LANES, dtype=jnp.int32)[:, None]
        small = jnp.zeros((24, max(length, model_width)), F32)
        shard = lax.axis_index("shard")
        place = lambda a, block, row: lax.dynamic_update_slice(
            a, block.astype(F32), (row, shard * block.shape[1])
        )
        small = place(small, jnp.stack([norm_self, norm_cross, norm_feed]), 0)
        small = place(small, block_ids, 3)
        small = place(small, bucket_bias, 8)
        held = forward(
            tokens[0],
            encoded[0],
            block_ids[0].astype(F32)[:, None],
            small,
            onehot.astype(BF16),
            (self_query, self_keyval, self_output, cross_query, cross_keyval, cross_output, feed_in, feed_out),
            reps,
            shards,
        )
        made = backward(tokens[0], cotangent[0], onehot.astype(BF16), held, reps, shards)
        sums = made.fin.transpose(0, 2, 1, 3).reshape(-1, model_width // shards, model_width)
        sums = sums.astype(F32)
        parts = feed_in.shape[1] // model_width
        inner = jnp.concatenate([sums[j] for j in range(parts)], axis=1)
        outer = sums[parts : 2 * parts].reshape(-1, model_width)
        co, ck, cv, cq, so, sk, sv, sq = (sums[2 * parts + i] for i in range(8))
        mine = lambda a, size: lax.dynamic_slice_in_dim(a, shard * size, size, a.ndim - 1)
        gains = mine(made.small_out[:3, :model_width], model_width // shards)
        table = mine(made.small_out[8 : 8 + heads, :bucket_count], bucket_count // shards)
        totals = (gains[0], sq, jnp.stack([sk, sv]), so, table)
        totals += (gains[1], cq, jnp.stack([ck, cv]), co, gains[2], inner, outer)
        return (held.result[None], made.d_tokens[None], made.d_memory[None]) + totals

    inputs = tokens[0].astype(F32)
    encoded_whole = gather(encoded[0])
    ids_whole = gather(block_ids[0])
    gains = gather(jnp.stack([norm_self, norm_cross, norm_feed]), 1).astype(F32)
    gain_first, gain_second, gain_third = gains[0:1], gains[1:2], gains[2:3]
    query_first, keyval_first, output_first, table = (
        gather(self_query),
        gather(self_keyval, 1),
        gather(self_output),
        gather(bucket_bias, 1),
    )
    query_second, keyval_second, output_second = (
        gather(cross_query),
        gather(cross_keyval, 1),
        gather(cross_output),
    )
    inner, outer = gather(feed_in), gather(feed_out)

    onehot = window_buckets[None, :] == jnp.arange(bucket_count, dtype=jnp.int32)[:, None]
    window = dot(table, onehot.astype(BF16)).reshape(heads // 2, 2, window_width)

    normed_first = (inputs * rms_scale(inputs) * gain_first).astype(BF16)
    normed_whole = gather(normed_first)
    query = dot(normed_first, query_first).astype(BF16)
    keys = dot(normed_whole, keyval_first[0]).astype(BF16)
    values = dot(normed_whole, keyval_first[1]).astype(BF16)
    attended, weights = attend(
        query, keys, values, (block_ids[0][:, None], ids_whole[None, :], window)
    )
    low_first = attended.astype(BF16)
    first = inputs + dot(low_first, output_first)

    memory_keys = dot(encoded_whole, keyval_second[0]).astype(BF16)
    memory_values = dot(encoded_whole, keyval_second[1]).astype(BF16)
    normed_second = (first * rms_scale(first) * gain_second).astype(BF16)
    query_cross = dot(normed_second, query_second).astype(BF16)
    attended_cross, weights_cross = attend(query_cross, memory_keys, memory_values)
    low_second = attended_cross.astype(BF16)
    second = first + dot(low_second, output_second)

    normed_third = (second * rms_scale(second) * gain_third).astype(BF16)
    preact = dot(normed_third, inner)
    value, slope = gelu_parts(preact)
    hidden = value.astype(BF16)
    result = (second + dot(hidden, outer)).astype(BF16)

    grad_result = cotangent[0]
    d_outer = dot_tn(hidden, grad_result)
    grad_preact = (dot_nt(grad_result, outer) * slope).astype(BF16)
    d_inner = dot_tn(normed_third, grad_preact)
    back, d_gain_third = rms_back(second, gain_third, dot_nt(grad_preact, inner))
    grad_second = grad_result.astype(F32) + back

    grad_second_low = grad_second.astype(BF16)
    d_output_second = dot_tn(low_second, grad_second_low)
    grad_att = dot_nt(grad_second_low, output_second).astype(BF16)
    d_query, d_keys, d_values = attend_back(
        query_cross, memory_keys, memory_values, weights_cross, attended_cross, grad_att
    )
    d_keyval_second = jnp.stack(
        [dot_tn(encoded_whole, d_keys), dot_tn(encoded_whole, d_values)]
    )
    d_memory = scatter(dot_nt(d_keys, keyval_second[0]) + dot_nt(d_values, keyval_second[1]))
    d_query_second = dot_tn(normed_second, d_query)
    back, d_gain_second = rms_back(first, gain_second, dot_nt(d_query, query_second))
    grad_first = grad_second + back

    grad_first_low = grad_first.astype(BF16)
    d_output_first = dot_tn(low_first, grad_first_low)
    grad_att = dot_nt(grad_first_low, output_first).astype(BF16)
    d_query, d_keys, d_values, d_window = attend_back(
        query, keys, values, weights, attended, grad_att, window.shape
    )
    d_table = lax.dot_general(
        d_window.reshape(heads, window_width),
        onehot.astype(F32),
        (((1,), (1,)), ((), ())),
        precision=lax.Precision.HIGHEST,
    )
    d_keyval_first = jnp.stack([dot_tn(normed_whole, d_keys), dot_tn(normed_whole, d_values)])
    grad_normed = scatter(
        dot_nt(d_keys, keyval_first[0]) + dot_nt(d_values, keyval_first[1])
    ).astype(F32) + dot_nt(d_query, query_first)
    d_query_first = dot_tn(normed_first, d_query)
    back, d_gain_first = rms_back(inputs, gain_first, grad_normed)
    d_inputs = grad_first + back

    gains = [d_gain_first, d_gain_second, d_gain_third]
    squares = [d_query_first, d_output_first, d_query_second, d_output_second]
    pairs = [d_keyval_first, d_keyval_second]
    total = lambda a, axis=0: lax.psum(scatter(a, axis), "rep").astype(F32)
    gains = [total(gain[0]) for gain in gains]
    squares = [total(square) for square in squares]
    pairs = [total(pair, 1) for pair in pairs]
    d_table, d_inner, d_outer = total(d_table, 1), total(d_inner), total(d_outer)
    totals = (gains[0], squares[0], pairs[0], squares[1], d_table)
    totals += (gains[1], squares[2], pairs[1], squares[3], gains[2], d_inner, d_outer)
    return (result[None], d_inputs[None], d_memory.astype(F32)[None]) + totals


def solution(mesh):
    rows, line = P("rep", "shard", None), P("shard")
    matrix, pair, table = P("shard", None), P(None, "shard", None), P(None, "shard")
    weights = (line, matrix, pair, matrix, table, line, matrix, pair, matrix, line, matrix, matrix)
    return jax.shard_map(
        layer,
        mesh=mesh,
        in_specs=(rows, rows, P("rep", "shard"), P(), rows) + weights,
        out_specs=(rows, rows, rows) + weights,
        check_vma=False,
    )
```

time: 5480 us -> 311 us (0.06)
  local copies, waits for them, and re-layouts: 4540 us -> 24.8 us
  waiting for transfers between devices: 576 us -> 0 us
  Pallas kernels: 0 us -> 272 us
  matrix products: 226 us -> 0 us
    gather x12 -> x0, local copies, waits for them, and re-layouts: 4350 us -> none  [bucket_onehot(): labels = jnp.take(buckets, offsets)]
    reduce_scatter x10 -> x0, waiting for transfers between devices: 319 us -> none  [the longest x1 50.6 us: shards(): lax.psum_scatter(d_outer.astype(jnp.bfloat16), 'shard', scatter_dimension...]
    pallas_call x0 -> x2, Pallas kernels: none -> 272 us  [the longest x1 173 us: backward(): pl.pallas_call(functools.partial(backward_kernel, reps, shards, names), i...]
    dot_general x60 -> x0, matrix products: 226 us -> none  [the longest x6 35.4 us: skew_bias(): jnp.einsum('id,duf->iuf', relative_bias_matrix.astype(jnp.float32), indic...]
    psum x1 -> x0, waiting for transfers between devices: 127 us -> none  [shards(): lax.psum(self_shares[2].astype(jnp.bfloat16), 'rep').astype(jnp.float32)]
    unnamed x25 -> x0, waiting for transfers between devices: 78.6 us -> none
    dot_general x6 -> x0, local copies, waits for them, and re-layouts: 55.5 us -> none  [skew_bias(): jnp.einsum('id,duf->iuf', relative_bias_matrix.astype(jnp.float32), indic...]
  transfers between devices with their start and end apart: 24 -> 0, of which waited for: 15 -> 0; matrix products, arithmetic and copies ran while one was open for 57% -> 0% of each run, Pallas kernels for 0% -> 0%
where the time goes in v1:
time: 311 us; the launch traced here: 305 us
  Pallas kernels  272 us (87%)
  local copies, waits for them, and re-layouts  24.8 us (8%)
  other arithmetic  6.69 us (2%)
    pallas_call x1, Pallas kernels, backward(): pl.pallas_call(functools.partial(backward_kernel, reps, shards, names), i...  173 us
    pallas_call x1, Pallas kernels, forward(): pl.pallas_call(functools.partial(forward_kernel, reps, shards, tuple(name...  99.1 us
    unnamed x22, local copies, waits for them, and re-layouts  8.5 us

profile of v1, /device:TPU:0, one launch (start us, length us, event | category | flops | bytes accessed | tf_op | source)
XLA Modules:
  0.0 304.6 jit_solution(2829418242118428753)
XLA Ops:
  0.7 0.7 stack.22
  1.3 0.7 stack.23
  2.0 0.7 stack.24
  2.6 0.7 fusion.3
  3.3 0.8 pad_dynamic-slice_fusion
  4.1 0.8 copy.48
  4.9 0.5 dynamic_update_slice.9
  5.4 0.3 dynamic_update_slice.10
  5.7 0.6 dynamic_update_slice.11.refs_3_
  6.3 0.0 copy-start.3
  6.3 0.8 copy.49.refs_2_
  7.1 0.8 fusion.refs_4_.refs_2_
  7.9 0.0 copy-done.3
  7.9 99.1 %shard_map.280 = (bf16[256,768]{1,0:T(8,128)(2,1)}, f32[256,768]{1,0:T(8,128)}, f32[256,768]{1,0:T(8,128)}, f32[2,6,256,128]{3,2,1,0:T(8,128)}, bf16[2,6,256,128...) custom-call(bf16[256,768]{1,0:T(8,128)(2,1)} %bitcast.60, ...), custom_call_target="tpu_custom_call" | custom-call | tf_op jit(solution)/shard_map/pallas_call | solution.py:928
  107.0 172.9 %shard_map.281 = (f32[256,768]{1,0:T(8,128)}, f32[256,768]{1,0:T(8,128)}, f32[24,768]{1,0:T(8,128)}, bf16[16,2,192,384]{3,2,1,0:T(8,128)(2,1)}) custom-call(bf16[256,768]{1,0:T(8,128)(2,1)} %bitcast.61, bf16[256,768]{1,0:T(8,128)(2,1)} %bitcast.70, bf16[128,1280]{1,0:T(8,128)(2,1)} %fusion.refs_4_.refs_2_, f32[24,1024]{1,0:T(8,128)} %get-tuple-element.36.refs_3_, ...), custom_call_target="tpu_custom_call" | custom-call | tf_op jit(solution)/shard_map/pallas_call | solution.py:1364
  279.9 0.7 slice.63
  280.6 0.7 slice.59
  281.4 0.6 fusion.2
  282.0 0.1 constant_dynamic-slice_fusion.1
  282.1 0.7 copy.61
  282.8 3.5 %convert_bitcast_fusion = f32[16,192,2,384]{3,1,2,0:T(8,128)S(1)} fusion(bf16[16,2,192,384]{3,2,1,0:T(8,128)(2,1)} %get-tuple-element.54), kind=kLoop, calls=%fused_computation | loop fusion | flops 2359296 | bytes 14155776 | tf_op jit(solution)/shard_map/convert_element_type | solution.py:1436
  286.3 0.2 slice.81
  286.5 2.0 copy.60
  288.5 1.6 copy.72
  290.1 0.2 slice_bitcast_fusion
  290.2 0.4 fusion.1
  290.6 0.5 copy.56
  291.2 1.1 copy.63
  292.3 0.5 copy.59
  292.8 0.5 copy.58
  293.3 0.5 copy.57
  293.8 1.7 pad_maximum_fusion
  295.5 0.5 copy.55
  296.0 0.9 copy.67
  296.8 0.5 copy.53
  297.3 0.9 copy.66
  298.1 0.5 copy.52
  298.6 0.9 copy.65
  299.4 0.5 copy.50
  299.9 0.0 copy-start.1
  299.9 0.9 copy.64
  300.8 1.1 copy.62
  301.9 0.0 copy-done.2
  301.9 0.7 copy.79
  302.6 0.0 copy-done.1
  302.6 0.9 copy.80
  303.5 0.0 copy-done
  303.5 0.9 copy.81
  (8 shorter events, 0.2 us)
Async XLA Ops:
  6.3 1.6 copy-start.3
  299.4 2.4 copy-start.2
  299.9 2.7 copy-start.1
  300.8 2.7 copy-start

commit v2 on v1

--- a/solution.py
+++ b/solution.py
@@ -18,7 +18,10 @@
 VMEM_LIMIT = 56 * 2**20
 FUSED_LIMIT = 62 * 2**20
 AHEAD = 2
+LATE = (1, 3)
+LATE_START = (-1, 1)
 SLOTS = 4
+LAG = 1
 MESH = pl.DeviceIdType.MESH
 
 
@@ -238,11 +241,12 @@
 
 class Place:
     def __init__(self, reps, shards):
-        self.nx, self.nz = shards // 2, reps // 2
+        self.nx, self.nh = shards // 2, reps // 4
         rep, shard = lax.axis_index("rep"), lax.axis_index("shard")
         self.rep, self.shard = rep, shard
         self.core, self.x = lax.rem(shard, 2), lax.div(shard, 2)
-        self.y, self.z = lax.rem(rep, 2), lax.div(rep, 2)
+        self.y, z = lax.rem(rep, 2), lax.div(rep, 2)
+        self.low, self.high = lax.rem(z, 2), lax.div(z, 2)
 
     def other_core(self):
         return (self.rep, self.x * 2 + 1 - self.core)
@@ -252,16 +256,19 @@
         return x, (self.rep, x * 2 + self.core)
 
     def other_y(self):
-        return (self.z * 2 + 1 - self.y, self.shard)
-
-    def z_at(self, step):
-        z = lax.rem(self.z + step, self.nz)
-        return z, (z * 2 + self.y, self.shard)
+        return (self.rep + 1 - 2 * self.y, self.shard)
+
+    def other_low(self):
+        return (self.rep + 2 - 4 * self.low, self.shard)
+
+    def high_at(self, step):
+        high = lax.rem(self.high + step, self.nh)
+        return high, (high * 4 + self.low * 2 + self.y, self.shard)
 
     def partners(self):
-        found = [self.other_core(), self.other_y()]
+        found = [self.other_core(), self.other_y(), self.other_low()]
         found += [self.x_at(d)[1] for d in range(1, self.nx)]
-        found += [self.z_at(d)[1] for d in range(1, self.nz)]
+        found += [self.high_at(d)[1] for d in range(1, self.nh)]
         return found
 
 
@@ -287,20 +294,30 @@
 
 
 class Reduction:
-    def __init__(self, place, recv_a, recv_b, recv_c, recv_d, fin, send, recv, own_sem):
-        self.place, self.recv_a, self.recv_b = place, recv_a, recv_b
-        self.recv_c, self.recv_d, self.fin = recv_c, recv_d, fin
+    def __init__(self, place, x_first, names, fin, parts, recv_x, recv_y, recv_low, recv_high, send, recv, own_sem):
+        self.place, self.x_first, self.parts, self.fin = place, x_first, parts, fin
+        self.names = names
+        self.recv_x, self.recv_y, self.recv_low, self.recv_high = recv_x, recv_y, recv_low, recv_high
         self.send, self.recv, self.own_sem = send, recv, own_sem
-        self.rows = recv_c.shape[1] // place.nz
+        self.half = parts.shape[3] // 2
+        self.rows = self.half // place.nh
+        stages = [self.over_y, self.over_low, self.over_high]
+        stages = [self.over_x] + stages if x_first else stages + [self.over_x]
+        stages += [self.back_high, self.back_low, self.back_y]
+        self.copies = stages
+        self.adds = stages.index(self.back_high)
 
     @staticmethod
-    def scratch(n, nx, nz, q, half):
-        copies = 3 + (nx - 1) + 2 * (nz - 1)
+    def scratch(n, x_first, nx, nh, q, half):
+        copies = 4 + nx + 2 * (nh - 1)
+        wide = (n,) if x_first else (n, nx)
+        x_part = (2, q) if x_first else (q // (2 * nh),)
         return [
             pltpu.VMEM((n, nx, 2, q, half), BF16),
-            pltpu.VMEM((n, nx - 1, 2, q, half), BF16),
-            pltpu.VMEM((n, q, half), BF16),
-            pltpu.VMEM((n, nz - 1, q // nz, half), BF16),
+            pltpu.VMEM((n, nx - 1) + x_part + (half,), BF16),
+            pltpu.VMEM(wide + (q, half), BF16),
+            pltpu.VMEM(wide + (q // 2, half), BF16),
+            pltpu.VMEM((n, nh - 1) + wide[1:] + (q // (2 * nh), half), BF16),
             pltpu.SemaphoreType.DMA((n, copies)),
             pltpu.SemaphoreType.DMA((n, copies)),
             pltpu.SemaphoreType.DMA((n,)),
@@ -309,94 +326,106 @@
     def copy(self, u, which, src, dst, device):
         return remote(src, dst, self.send.at[u, which], self.recv.at[u, which], device)
 
-    def copies_a(self, u, src):
-        return [self.copy(u, 0, src, self.recv_a.at[u], self.place.other_core())]
-
-    def copies_b(self, u):
-        p = self.place
-        out = []
+    def low_rows(self, low):
+        return pl.ds(pl.multiple_of(low * self.half, 16), self.half)
+
+    def high_rows(self, high):
+        at = self.place.low * self.half + high * self.rows
+        return pl.ds(pl.multiple_of(at, 16), self.rows)
+
+    def chips(self):
+        return self.place.x if self.x_first else slice(None)
+
+    def over_core(self, u, src):
+        return [self.copy(u, 0, src, self.parts.at[u], self.place.other_core())]
+
+    def over_x(self, u):
+        p, out = self.place, []
+        rest = () if self.x_first else (p.y, self.high_rows(p.high))
         for d in range(1, p.nx):
             x, device = p.x_at(d)
-            out.append(self.copy(u, 2 + d, self.recv_a.at[u, x], self.recv_b.at[u, d - 1], device))
-        return out
-
-    def copies_c(self, u):
-        p = self.place
-        return [self.copy(u, 1, self.recv_b.at[u, 0, 1 - p.y], self.recv_c.at[u], p.other_y())]
-
-    def copies_d(self, u):
-        p, out = self.place, []
-        for d in range(1, p.nz):
-            z, device = p.z_at(d)
-            src = self.recv_c.at[u, pl.ds(pl.multiple_of(z * self.rows, self.rows), self.rows)]
-            out.append(self.copy(u, 1 + p.nx + d, src, self.recv_d.at[u, d - 1], device))
-        return out
+            src = self.parts.at[(u, x) + rest]
+            out.append(self.copy(u, 2 + d, src, self.recv_x.at[u, d - 1], device))
+        return out, (u, p.x) + rest, [self.recv_x.at[u, d] for d in range(p.nx - 1)]
+
+    def over_y(self, u):
+        p, chips = self.place, self.chips()
+        src = self.parts.at[u, chips, 1 - p.y]
+        copies = [self.copy(u, 1, src, self.recv_y.at[u], p.other_y())]
+        return copies, (u, chips, p.y), [self.recv_y.at[u]]
+
+    def over_low(self, u):
+        p, chips = self.place, self.chips()
+        src = self.parts.at[u, chips, p.y, self.low_rows(1 - p.low)]
+        copies = [self.copy(u, 2 + p.nx, src, self.recv_low.at[u], p.other_low())]
+        return copies, (u, chips, p.y, self.low_rows(p.low)), [self.recv_low.at[u]]
+
+    def over_high(self, u):
+        p, chips, out = self.place, self.chips(), []
+        for d in range(1, p.nh):
+            high, device = p.high_at(d)
+            src = self.parts.at[u, chips, p.y, self.high_rows(high)]
+            out.append(self.copy(u, 3 + p.nx + d, src, self.recv_high.at[u, d - 1], device))
+        came = [self.recv_high.at[u, d] for d in range(p.nh - 1)]
+        return out, (u, chips, p.y, self.high_rows(p.high)), came
 
     def piece(self, u):
         p = self.place
-        rows = pl.ds(pl.multiple_of(p.z * self.rows, self.rows), self.rows)
-        return self.recv_c.at[u, rows], self.fin.at[u, p.y, rows]
-
-    def copies_e(self, u):
-        p, out = self.place, []
-        for d in range(1, p.nz):
-            out.append(self.copy(u, p.nx + p.nz + d, *self.piece(u), p.z_at(d)[1]))
-        return out
+        rows = self.high_rows(p.high)
+        return self.parts.at[u, p.x, p.y, rows], self.fin.at[self.names[u], p.y, rows]
 
     def keep(self, u):
         return pltpu.make_async_copy(*self.piece(u), self.own_sem.at[u])
 
-    def copies_f(self, u):
+    def back_high(self, u):
         p = self.place
-        return [self.copy(u, 2, self.fin.at[u, p.y], self.fin.at[u, p.y], p.other_y())]
-
-    def start(self, copies):
-        for copy in copies:
-            copy.start()
-
-    def arrived(self, copies):
-        for copy in copies:
-            copy.wait_recv()
+        return [
+            self.copy(u, 2 + p.nx + p.nh + d, *self.piece(u), p.high_at(d)[1])
+            for d in range(1, p.nh)
+        ]
+
+    def back_low(self, u):
+        p = self.place
+        rows = self.fin.at[self.names[u], p.y, self.low_rows(p.low)]
+        return [self.copy(u, 3 + p.nx, rows, rows, p.other_low())]
+
+    def back_y(self, u):
+        half = self.fin.at[self.names[u], self.place.y]
+        return [self.copy(u, 2, half, half, self.place.other_y())]
 
     def begin(self, u, src):
-        self.start(self.copies_a(u, src))
+        self.over_core(u, src)[0].start()
 
     def collect(self, u, src, own):
-        self.arrived(self.copies_a(u, src))
-        self.recv_a[u] = added(self.recv_a[u], own[...]).astype(BF16)
-
-    def step_c(self, u):
-        p = self.place
-        self.arrived(self.copies_b(u))
-        parts = [self.recv_a[u, p.x]] + [self.recv_b[u, d] for d in range(p.nx - 1)]
-        self.recv_b[u, 0] = added(*parts).astype(BF16)
-        self.start(self.copies_c(u))
-
-    def step_d(self, u):
-        self.arrived(self.copies_c(u))
-        self.recv_c[u] = added(self.recv_b[u, 0, self.place.y], self.recv_c[u]).astype(BF16)
-        self.start(self.copies_d(u))
-
-    def step_e(self, u):
-        p = self.place
-        self.arrived(self.copies_d(u))
-        rows = pl.ds(pl.multiple_of(p.z * self.rows, self.rows), self.rows)
-        parts = [self.recv_c[u, rows]] + [self.recv_d[u, d] for d in range(p.nz - 1)]
-        self.recv_c[u, rows] = added(*parts).astype(BF16)
-        self.start(self.copies_e(u))
-        self.keep(u).start()
-
-    def step_f(self, u):
-        self.arrived(self.copies_e(u))
-        self.keep(u).wait()
-        self.start(self.copies_f(u))
-
-    def step_g(self, u):
-        self.arrived(self.copies_f(u))
-
-    def sent_rest(self, u):
-        for copies in (self.copies_b(u), self.copies_c(u), self.copies_d(u), self.copies_e(u), self.copies_f(u)):
+        self.over_core(u, src)[0].wait_recv()
+        self.parts[u] = added(self.parts[u], own[...]).astype(BF16)
+
+    def start(self, u, stage):
+        if stage < len(self.copies):
+            copies = self.copies[stage](u)
+            for copy in copies[0] if stage < self.adds else copies:
+                copy.start()
+
+    def step(self, u, stage):
+        if stage < self.adds:
+            copies, stays, came = self.copies[stage](u)
             for copy in copies:
+                copy.wait_recv()
+            total = added(self.parts[stays], *[part[...] for part in came])
+            self.parts[stays] = total.astype(BF16)
+            if stage + 1 == self.adds:
+                self.keep(u).start()
+        else:
+            for copy in self.copies[stage](u):
+                copy.wait_recv()
+            if stage == self.adds:
+                self.keep(u).wait()
+        self.start(u, stage + 1)
+
+    def sent(self, u):
+        for stage in range(len(self.copies)):
+            copies = self.copies[stage](u)
+            for copy in copies[0] if stage < self.adds else copies:
                 copy.wait_send()
 
 
@@ -406,10 +435,10 @@
         self.send, self.recv = send, recv
 
     @staticmethod
-    def scratch(nx, nz, shape):
-        copies = 2 + nx - 1 + nz - 1
+    def scratch(nx, nh, shape):
+        copies = 3 + nx - 1 + nh - 1
         return [
-            pltpu.VMEM((5,) + shape, F32),
+            pltpu.VMEM((6,) + shape, F32),
             pltpu.VMEM((copies,) + shape, F32),
             pltpu.SemaphoreType.DMA((copies,)),
             pltpu.SemaphoreType.DMA((copies,)),
@@ -417,12 +446,13 @@
 
     def copies(self, stage):
         p = self.place
-        first, devices = {
-            0: (0, [p.other_core()]),
-            1: (2, [p.x_at(d)[1] for d in range(1, p.nx)]),
-            2: (1, [p.other_y()]),
-            3: (1 + p.nx, [p.z_at(d)[1] for d in range(1, p.nz)]),
-        }[stage]
+        first, devices = [
+            (0, [p.other_core()]),
+            (3, [p.x_at(d)[1] for d in range(1, p.nx)]),
+            (1, [p.other_y()]),
+            (2, [p.other_low()]),
+            (2 + p.nx, [p.high_at(d)[1] for d in range(1, p.nh)]),
+        ][stage]
         return [
             remote(self.held.at[stage], self.landed.at[first + i], self.send.at[first + i], self.recv.at[first + i], device)
             for i, device in enumerate(devices)
@@ -436,7 +466,7 @@
         for copy in self.copies(0)[0]:
             copy.start()
 
-    def step(self, stage, stages=4):
+    def step(self, stage, stages=5):
         copies, slots = self.copies(stage)
         for copy in copies:
             copy.wait_recv()
@@ -449,7 +479,7 @@
                 copy.start()
         return total
 
-    def sent(self, stages=4):
+    def sent(self, stages=5):
         for stage in range(stages):
             for copy in self.copies(stage)[0]:
                 copy.wait_send()
@@ -646,6 +676,13 @@
     return merge_heads(dot(p_ref[...], values_ref[...]))
 
 
+def bucket_onehot(buckets_ref, place, rows, length):
+    start = length - rows - place.shard * rows
+    window = buckets_ref[:, pl.ds(pl.multiple_of(start, LANES), length + rows)]
+    which = lax.broadcasted_iota(jnp.int32, (LANES, length + rows), 0)
+    return jnp.where(window == which, 1.0, 0.0)
+
+
 def forward_kernel(reps, shards, names, *refs):
     r = types.SimpleNamespace(**dict(zip(names, refs)))
     place = Place(reps, shards)
@@ -684,8 +721,23 @@
     def gain(i):
         return r.small_held[2, i : i + 1, :width]
 
+    shard = place.shard
+    wide = r.small_held.shape[2]
+    sub = lax.broadcasted_iota(jnp.int32, (8, wide), 0)
+    padded = lambda a: jnp.concatenate([a, jnp.zeros((a.shape[0], wide - a.shape[1]), F32)], axis=1)
+    shifted = lambda a, by: pltpu.roll(padded(a), shard * by, 1)
+    ids = r.ids[...].astype(F32)
+    gains = [gain_ref[...].astype(F32).reshape(1, q) for gain_ref in (r.norm_self, r.norm_cross, r.norm_feed)]
+    mine = jnp.concatenate(gains + [jnp.zeros((5, q), F32)], axis=0)
+    mine = jnp.where(sub == 3, 0.0, shifted(mine, q))
+    mine = mine + jnp.where(sub == 3, shifted(jnp.broadcast_to(ids, (8, rows)), rows), 0.0)
+    table = r.bucket_bias[...].astype(F32).T
+    heads, cut = table.shape
+    table = jnp.concatenate([table, jnp.zeros((16 - heads, cut), F32)], axis=0)
+    r.small_held[0] = jnp.concatenate([mine, shifted(table, cut)], axis=0)
+    r.row_ids[...] = jnp.broadcast_to(ids, (8, rows)).T[:, 0:1]
     enter(place)
-    small.begin(r.small_in[...])
+    small.launch()
     line = [(gather, (u,)) for u in (1, 2, 0)] + [(tokens, ()), (memories, ())]
     line += [(gather, (u,)) for u in [3, 5, 6, 4, 7] + list(range(8, units))]
 
@@ -703,7 +755,7 @@
     gathered = small.step(1, 2)
     r.small_out[...] = gathered
     table = gathered[8:24, :LANES].astype(BF16)
-    biases = dot(table, r.onehot[...])
+    biases = dot(table, bucket_onehot(r.buckets, place, rows, length).astype(BF16))
     for i in range(pairs):
         r.window[i] = biases[2 * i : 2 * i + 2]
     for u in (1, 2, 0):
@@ -877,7 +929,7 @@
     emit_enc.wait()
 
 
-def forward(tokens, encoded, row_ids, small, onehot, shards_of, reps, shards):
+def forward(tokens, encoded, ids, buckets, gains, bucket_bias, shards_of, reps, shards):
     rows, width = tokens.shape
     length, memory = rows * shards, encoded.shape[0] * shards
     nx = shards // 2
@@ -885,6 +937,7 @@
     hidden = feed_in.shape[1]
     units = 8 + 2 * (hidden // width)
     pairs = width // LANES
+    small = (24, max(length, width))
     kept = lambda *shape, dtype=BF16: (pl.BlockSpec(memory_space=pl.ANY), jax.ShapeDtypeStruct(shape, dtype))
     near = lambda *shape, dtype=F32: (pl.BlockSpec(memory_space=pltpu.VMEM), jax.ShapeDtypeStruct(shape, dtype))
     outs = dict(
@@ -893,7 +946,7 @@
         second_out=near(rows, width),
         low_out=near(2, pairs, rows, LANES),
         q_out=near(2, pairs, rows, LANES, dtype=BF16),
-        small_out=near(*small.shape),
+        small_out=near(*small),
         low_t=near(2, width, rows, dtype=BF16),
         normed2_t=near(width, rows, dtype=BF16),
         normed3_t=near(width, rows, dtype=BF16),
@@ -910,7 +963,8 @@
         tok=pltpu.VMEM((length, width), BF16),
         enc=pltpu.VMEM((memory, width), BF16),
         kv=pltpu.VMEM((4, pairs, length, LANES), BF16),
-        window=pltpu.VMEM((pairs, 2, onehot.shape[1]), F32),
+        window=pltpu.VMEM((pairs, 2, length + rows), F32),
+        row_ids=pltpu.VMEM((rows, 1), F32),
         probs=pltpu.VMEM((2, 2 * rows, length), BF16),
         normed=pltpu.VMEM((rows, width), BF16),
         hidden=pltpu.VMEM((hidden // width, rows, width), BF16),
@@ -919,22 +973,23 @@
         p_sem=pltpu.SemaphoreType.DMA((2,)),
         out_sem=pltpu.SemaphoreType.DMA((units + 6,)),
     )
-    scratch.update(zip(("small_held", "small_landed", "small_send", "small_recv"), SmallSum.scratch(nx, reps // 2, small.shape)))
+    scratch.update(zip(("small_held", "small_landed", "small_send", "small_recv"), SmallSum.scratch(nx, reps // 4, small)))
     scratch.update(zip(("w_send", "w_recv", "w_own"), Gather.scratch(units, nx)))
     scratch.update(zip(("t_send", "t_recv", "t_own"), Spread.scratch(nx)))
     scratch.update(zip(("e_send", "e_recv", "e_own"), Spread.scratch(nx)))
     shard_names = ["self_query", "self_keyval", "self_output", "cross_query", "cross_keyval", "cross_output", "feed_in", "feed_out"]
-    names = ["tok_in", "enc_in", "row_ids", "small_in", "onehot"] + shard_names + list(outs) + list(scratch)
+    near_names = ["tok_in", "enc_in", "ids", "buckets", "norm_self", "norm_cross", "norm_feed", "bucket_bias"]
+    names = near_names + shard_names + list(outs) + list(scratch)
     made = pl.pallas_call(
         functools.partial(forward_kernel, reps, shards, tuple(names)),
-        in_specs=[pl.BlockSpec(memory_space=pltpu.VMEM)] * 5 + [pl.BlockSpec(memory_space=pl.ANY)] * 8,
+        in_specs=[pl.BlockSpec(memory_space=pltpu.VMEM)] * 8 + [pl.BlockSpec(memory_space=pl.ANY)] * 8,
         out_specs=[spec for spec, _ in outs.values()],
         out_shape=[shape for _, shape in outs.values()],
         scratch_shapes=list(scratch.values()),
         compiler_params=pltpu.CompilerParams(
             collective_id=2, has_side_effects=True, vmem_limit_bytes=FUSED_LIMIT
         ),
-    )(tokens, encoded, row_ids, small, onehot, *shards_of)
+    )(tokens, encoded, ids, buckets, *gains, bucket_bias, *shards_of)
     return types.SimpleNamespace(**dict(zip(outs, made)))
 
 
@@ -1019,6 +1074,13 @@
     return d_query, d_keys, d_values, windows
 
 
+REDUCTION = ("_parts", "_x", "_y", "_low", "_high", "_send", "_recv", "_own")
+
+
+def late_units(units):
+    return [n for n in LATE if n < units]
+
+
 def backward_kernel(reps, shards, names, *refs):
     r = types.SimpleNamespace(**dict(zip(names, refs)))
     place = Place(reps, shards)
@@ -1028,7 +1090,17 @@
     q = width // shards
     part = r.hidden_t.shape[0] // width
     units = 8 + 2 * part
-    red = Reduction(place, r.recv_a, r.recv_b, r.recv_c, r.recv_d, r.fin, r.r_send, r.r_recv, r.r_own)
+    late = late_units(units)
+    order = [n for n in range(units) if n not in late]
+    reductions = [
+        Reduction(place, x_first, names, r.fin, *(getattr(r, name + end) for end in REDUCTION))
+        for x_first, names, name in ((True, order, "a"), (False, late, "b"))
+    ]
+    stages = len(reductions[0].copies)
+
+    def owner(n):
+        return (reductions[1], late.index(n)) if n in late else (reductions[0], order.index(n))
+
     small = SmallSum(place, r.small_held, r.small_landed, r.small_send, r.small_recv)
     sum_memory = RowSum(place, r.m_parts, r.m_a, r.m_b, r.m_send, r.m_recv)
     sum_tokens = RowSum(place, r.m_parts, r.t_a, r.t_b, r.t_send, r.t_recv)
@@ -1041,7 +1113,7 @@
         return pltpu.make_async_copy(r.w_in.at[block], r.w.at[slot], r.w_sem.at[slot])
 
     def load_slope(j):
-        slot = lax.rem(j, 2)
+        slot = j % 2
         return pltpu.make_async_copy(r.slope.at[j], r.slopes.at[slot], r.s_sem.at[slot])
 
     def load_kv(i, slot):
@@ -1055,10 +1127,10 @@
         return pltpu.make_async_copy(source, r.rows_t, r.t_sem.at[which])
 
     def away(n):
-        return r.made.at[lax.rem(n, SLOTS), 1 - place.core]
+        return r.made.at[n % SLOTS, 1 - place.core]
 
     def fill(n, value):
-        slot = lax.rem(n, SLOTS)
+        slot = n % SLOTS
         rest = value.shape[0] // shards
         half = width // 2
         for s in range(shards):
@@ -1066,22 +1138,43 @@
                 r.made[slot, s % 2, s // 2, h] = value[
                     s * rest : (s + 1) * rest, h * half : (h + 1) * half
                 ].astype(BF16)
-        red.begin(n, away(n))
+        red, u = owner(n)
+        red.begin(u, away(n))
+
+    def left(n):
+        red, u = owner(n)
+        red.over_core(u, away(n))[0].wait_send()
 
     def free(n):
-        red.copies_a(n - SLOTS, away(n))[0].wait_send()
+        if n >= SLOTS:
+            left(n - SLOTS)
 
     def take(n):
-        red.collect(n, away(n), r.made.at[lax.rem(n, SLOTS), place.core])
-
-    def advance(n):
-        if n < units:
-            red.step_c(n)
-            if n + AHEAD < units:
-                red.start(red.copies_b(n + AHEAD))
-        for late, step in ((1, red.step_d), (2, red.step_e), (3, red.step_f), (4, red.step_g)):
-            if 0 <= n - late < units:
-                step(n - late)
+        red, u = owner(n)
+        red.collect(u, away(n), r.made.at[n % SLOTS, place.core])
+        if n in late:
+            red.start(u, 0)
+        elif order.index(n) < AHEAD:
+            red.start(u, 0)
+
+    done_stages = {n: 0 for n in range(units)}
+
+    def move(n, upto):
+        red, u = owner(n)
+        while done_stages[n] < min(upto, stages):
+            red.step(u, done_stages[n])
+            done_stages[n] += 1
+
+    def advance(t):
+        for back in range(stages):
+            at = t - back
+            if 0 <= at < len(order):
+                move(order[at], back + 1)
+            if back == 0 and 0 <= t + AHEAD < len(order):
+                red, u = owner(order[t + AHEAD])
+                red.start(u, 0)
+        for i, n in enumerate(late):
+            move(n, t - LATE_START[i])
 
     enter(place)
     load_slope(0).start()
@@ -1093,61 +1186,42 @@
     load_t(r.enc_t, 0).start()
     r.acc[...] = jnp.zeros((rows, width), F32)
 
-    def feed(j, carry):
-        slot = 2 * lax.rem(j, 2)
+    for j in range(part):
+        slot = 2 * (j % 2)
         load_weight(8, slot).wait()
         load_weight(8 + part, slot + 1).wait()
         load_slope(j).wait()
-
-        @pl.when(j + 1 < part)
-        def _():
+        if j + 1 < part:
             load_slope(j + 1).start()
             load_weight(8 + j + 1, 2 - slot).start()
             load_weight(8 + part + j + 1, 3 - slot).start()
-
         grad_hidden = dot_nt(r.cotangent[...], r.w[slot + 1])
-        grad = (grad_hidden * r.slopes[lax.rem(j, 2)]).astype(BF16)
+        grad = (grad_hidden * r.slopes[j % 2]).astype(BF16)
+        free(j)
         fill(j, dot(r.normed3_t[...], grad))
         r.acc[...] += dot_nt(grad, r.w[slot])
-
-        @pl.when(j >= 1)
-        def _():
+        if j >= 1:
             take(j - 1)
-
-        return carry
-
-    lax.fori_loop(0, part, feed, 0)
     for slot, u in ((0, 7), (1, 5), (2, 6), (3, 4)):
         load_weight(u, slot).start()
     take(part - 1)
-    for n in range(AHEAD):
-        red.start(red.copies_b(n))
-
-    def feed_out(m, carry):
+    for m in range(part):
         n = part + m
         free(n)
         value = jnp.concatenate(
             [
-                dot(
-                    r.hidden_t[pl.ds(pl.multiple_of(s * width + m * q, 16), q), :],
-                    r.cotangent[...],
-                )
+                dot(r.hidden_t[s * width + m * q : s * width + (m + 1) * q, :], r.cotangent[...])
                 for s in range(shards)
             ],
             axis=0,
         )
         fill(n, value)
-
-        @pl.when(m >= 1)
-        def _():
+        if m >= 1:
             take(n - 1)
-
-        return carry
-
-    lax.fori_loop(0, part, feed_out, 0)
     back, d_gain3 = rms_back(r.second[...], gain(2), r.acc[...])
     r.grad[...] = r.cotangent[...].astype(F32) + back
     take(2 * part - 1)
+    advance(0)
 
     def attention(which, fold, steps):
         def pair(i, carry):
@@ -1161,7 +1235,7 @@
                 r.low[which, i],
                 r.grad_att[i],
                 r.ds,
-                r.onehot.shape[1] if fold else None,
+                length + rows if fold else None,
             )
             r.d_query[i] = d_query
             at = pl.ds(pl.multiple_of(i * LANES, LANES), LANES)
@@ -1200,7 +1274,7 @@
     take(n)
     for slot in range(2):
         load_kv(2 + slot, slot).wait()
-    attention(1, False, [(0, 0), (4, 1)])
+    attention(1, False, [(1, 1), (5, 2)])
     for slot in range(2):
         load_kv(slot, slot).start()
         load_p(0, slot).start()
@@ -1216,6 +1290,7 @@
     free(n + 2)
     fill(n + 2, dot_nt(r.rows_t[...], r.dv_t[...]))
     take(n + 1)
+    advance(3)
     load_t(r.tok_t, 1).start()
     d_query = joined_query()
     load_weight(4, 3).wait()
@@ -1225,7 +1300,7 @@
     fill(n + 3, dot(r.normed2_t[...], d_query))
     take(n + 2)
     r.grad[...] = r.grad[...] + back
-    advance(2)
+    advance(4)
 
     grad_low = r.grad[...].astype(BF16)
     take(n + 3)
@@ -1236,7 +1311,7 @@
     take(n + 4)
     for slot in range(2):
         load_kv(slot, slot).wait()
-    attention(0, True, [(1, 3), (4, 4)])
+    attention(0, True, [(2, 5), (5, 6)])
     load_weight(1, 1).wait()
     load_weight(2, 2).wait()
     sum_memory.to_core().wait_send()
@@ -1249,7 +1324,7 @@
     fill(n + 6, dot_nt(r.rows_t[...], r.dv_t[...]))
     take(n + 5)
     r.d_memory[...] = sum_memory.finish().T
-    advance(5)
+    advance(7)
     d_query = joined_query()
     free(n + 7)
     mine = pl.ds(pl.multiple_of(place.shard * rows, LANES), rows)
@@ -1260,13 +1335,13 @@
     windows = jnp.concatenate([r.d_window[i] for i in range(pairs)], axis=0)
     d_table = lax.dot_general(
         windows,
-        r.onehot[...].astype(F32),
+        bucket_onehot(r.buckets, place, rows, length),
         (((1,), (1,)), ((), ())),
         precision=lax.Precision.HIGHEST,
         preferred_element_type=F32,
     )
     take(n + 7)
-    advance(6)
+    advance(8)
     values = r.tokens[...].astype(F32)
     back, d_gain1 = rms_back(values, gain(0), r.acc[...] + sum_tokens.finish().T)
     r.d_tokens[...] = r.grad[...] + back
@@ -1275,25 +1350,28 @@
         r.small_held[0, i : i + 1, :width] = d_gain
     r.small_held[0, 8 : 8 + 2 * pairs, :LANES] = d_table
     small.launch()
-    for n in range(7, units + 4):
-        advance(n)
-        if n < 11:
-            small.step(n - 7)
-    r.small_out[...] = r.small_held[4]
+    for t in range(9, len(order) + stages):
+        advance(t)
+        if t < 14:
+            small.step(t - 9)
+    for n in range(units):
+        move(n, stages)
+    r.small_out[...] = r.small_held[5]
     for n in range(units):
         if n >= units - SLOTS:
-            red.copies_a(n, away(n))[0].wait_send()
-        red.sent_rest(n)
+            left(n)
+        red, u = owner(n)
+        red.sent(u)
     small.sent()
     sum_tokens.to_core().wait_send()
     sum_memory.sent()
     sum_tokens.sent()
 
 
-def backward(tokens, cotangent, onehot, held, reps, shards):
+def backward(tokens, cotangent, buckets, held, reps, shards):
     rows, width = tokens.shape
     length = held.enc_out.shape[1]
-    nx, nz = shards // 2, reps // 2
+    nx, nh = shards // 2, reps // 4
     pairs = width // LANES
     q, half = width // shards, width // 2
     units = held.w_out.shape[0] // width
@@ -1303,7 +1381,7 @@
     ins = dict(
         tokens=(near, tokens),
         cotangent=(near, cotangent),
-        onehot=(near, onehot),
+        buckets=(near, buckets),
         gains=(near, held.small_out),
         first=(near, held.first_out),
         second=(near, held.second_out),
@@ -1336,7 +1414,7 @@
         dv_t=pltpu.VMEM((width, length), BF16),
         d_query=pltpu.VMEM((pairs, rows, LANES), BF16),
         grad_att=pltpu.VMEM((pairs, rows, LANES), BF16),
-        d_window=pltpu.VMEM((pairs, 2, onehot.shape[1]), F32),
+        d_window=pltpu.VMEM((pairs, 2, length + rows), F32),
         acc=pltpu.VMEM((rows, width), F32),
         grad=pltpu.VMEM((rows, width), F32),
         made=pltpu.VMEM((SLOTS, 2, nx, 2, q, half), BF16),
@@ -1347,14 +1425,12 @@
         p_sem=pltpu.SemaphoreType.DMA((2,)),
         t_sem=pltpu.SemaphoreType.DMA((2,)),
     )
+    counts = {"a": units - len(late_units(units)), "b": len(late_units(units))}
+    for name, count in counts.items():
+        made_for = Reduction.scratch(count, name == "a", nx, nh, q, half)
+        scratch.update(zip((name + end for end in REDUCTION), made_for))
     scratch.update(
-        zip(
-            ("recv_a", "recv_b", "recv_c", "recv_d", "r_send", "r_recv", "r_own"),
-            Reduction.scratch(units, nx, nz, q, half),
-        )
-    )
-    scratch.update(
-        zip(("small_held", "small_landed", "small_send", "small_recv"), SmallSum.scratch(nx, nz, small))
+        zip(("small_held", "small_landed", "small_send", "small_recv"), SmallSum.scratch(nx, nh, small))
     )
     for name in "mt":
         keys = (name + end for end in ("_parts", "_a", "_b", "_send", "_recv"))
@@ -1374,8 +1450,85 @@
     return types.SimpleNamespace(**dict(zip(outs, made)))
 
 
+def finish_kernel(squares, shards, names, *refs):
+    r = types.SimpleNamespace(**dict(zip(names, refs)))
+    step = pl.program_id(0)
+    shard = lax.axis_index("shard")
+    whole = lambda ref: jnp.concatenate([ref[0, 0], ref[0, 1]], axis=1).astype(F32)
+    r.feed_in[...] = whole(r.fin_in)
+    r.feed_out[...] = whole(r.fin_out)
+    for source, group in zip((r.fin_cross, r.fin_self), squares):
+        value = whole(source)
+        for name, first, count in group:
+            out = getattr(r, name)
+
+            @pl.when((step >= first) & (step < first + count))
+            def _():
+                out[...] = value.reshape(out.shape)
+
+    r.d_tokens[...] = r.tokens_in[...]
+    r.d_memory[...] = r.memory_in[...]
+    r.result[...] = r.result_in[...]
+
+    @pl.when(step == 0)
+    def _():
+        small = r.small[...]
+        width = small.shape[1]
+        mine = lambda by: pltpu.roll(small, lax.rem(width - shard * by, width), 1)
+        gains = mine(width // shards)
+        for i, out in enumerate((r.norm_self, r.norm_cross, r.norm_feed)):
+            out[...] = gains[i : i + 1, : width // shards].reshape(out.shape)
+        cut, heads = r.bucket_bias.shape
+        r.bucket_bias[...] = mine(cut)[8:24, :LANES].T[:cut, :heads]
+
+
+def finish(made, result, table_shape, shards):
+    units, _, q, half = made.fin.shape
+    rows, width = made.d_tokens.shape
+    steps = units // 4
+    still = lambda *shape: pl.BlockSpec(shape, lambda n: (0,) * len(shape))
+    line = pl.BlockSpec((rows // steps, width), lambda n: (n, 0))
+    unit = lambda group: pl.BlockSpec((1, 2, q, half), lambda n: (group * steps + n, 0, 0, 0))
+    pair = lambda first: pl.BlockSpec((1, q, width), lambda n: (jnp.where(n <= first, 0, 1), 0, 0))
+    squares = (
+        (("cross_output", 0, 1), ("cross_keyval", 1, 2), ("cross_query", 3, 1)),
+        (("self_output", 0, 1), ("self_keyval", 1, 2), ("self_query", 3, 1)),
+    )
+    square = ((q, width), still(q, width))
+    outs = dict(
+        feed_in=((q, steps * width), pl.BlockSpec((q, width), lambda n: (0, n))),
+        feed_out=((steps * q, width), pl.BlockSpec((q, width), lambda n: (n, 0))),
+        cross_output=square,
+        cross_keyval=((2, q, width), pair(1)),
+        cross_query=square,
+        self_output=square,
+        self_keyval=((2, q, width), pair(1)),
+        self_query=square,
+        d_tokens=((rows, width), line),
+        d_memory=((rows, width), line),
+        result=((rows, width), line),
+        norm_self=((q,), still(q)),
+        norm_cross=((q,), still(q)),
+        norm_feed=((q,), still(q)),
+        bucket_bias=(table_shape, still(*table_shape)),
+    )
+    names = ("fin_in", "fin_out", "fin_cross", "fin_self", "tokens_in", "memory_in", "result_in", "small")
+    done = pl.pallas_call(
+        functools.partial(finish_kernel, squares, shards, names + tuple(outs)),
+        grid=(steps,),
+        in_specs=[unit(0), unit(1), unit(2), unit(3), line, line, line, still(*made.small_out.shape)],
+        out_specs=[spec for _, spec in outs.values()],
+        out_shape=[
+            jax.ShapeDtypeStruct(shape, BF16 if name == "result" else F32)
+            for name, (shape, _) in outs.items()
+        ],
+        compiler_params=pltpu.CompilerParams(vmem_limit_bytes=VMEM_LIMIT),
+    )(*[made.fin] * 4, made.d_tokens, made.d_memory, result, made.small_out)
+    return types.SimpleNamespace(**dict(zip(outs, done)))
+
+
 def tiles_evenly(reps, shards, width):
-    if reps % 2 or shards % 2 or width % shards:
+    if reps % 4 or shards % 2 or width % shards:
         return False
     return (width // shards) % (8 * reps) == 0 and width % (4 * HD) == 0
 
@@ -1406,44 +1559,36 @@
     row_anchor = lax.axis_index("shard") * positions
     heads, bucket_count = bucket_bias.shape[0], bucket_bias.shape[1] * shards
     window_width = length + positions
-    window_buckets = lax.dynamic_slice_in_dim(
-        jnp.pad(buckets, (1, 0)), length - row_anchor - positions, window_width
-    )
     fused = tiles_evenly(reps, shards, model_width) and encoded.shape == tokens.shape
-    fused = fused and feed_out.shape[0] == model_width and positions % LANES == 0
+    fused = fused and feed_out.shape[0] == model_width
+    fused = fused and feed_in.shape[1] == 4 * model_width and positions % LANES == 0
     if fused:
-        onehot = window_buckets[None, :] == jnp.arange(LANES, dtype=jnp.int32)[:, None]
-        small = jnp.zeros((24, max(length, model_width)), F32)
-        shard = lax.axis_index("shard")
-        place = lambda a, block, row: lax.dynamic_update_slice(
-            a, block.astype(F32), (row, shard * block.shape[1])
+        offsets = jnp.pad(buckets, (1, 0))[None, :]
+        gains = (norm_self, norm_cross, norm_feed)
+        matrices = (self_query, self_keyval, self_output, cross_query, cross_keyval, cross_output)
+        matrices += (feed_in, feed_out)
+        held = forward(
+            tokens[0], encoded[0], block_ids, offsets, gains, bucket_bias.T, matrices, reps, shards
         )
-        small = place(small, jnp.stack([norm_self, norm_cross, norm_feed]), 0)
-        small = place(small, block_ids, 3)
-        small = place(small, bucket_bias, 8)
-        held = forward(
-            tokens[0],
-            encoded[0],
-            block_ids[0].astype(F32)[:, None],
-            small,
-            onehot.astype(BF16),
-            (self_query, self_keyval, self_output, cross_query, cross_keyval, cross_output, feed_in, feed_out),
-            reps,
-            shards,
+        made = backward(tokens[0], cotangent[0], offsets, held, reps, shards)
+        out = finish(made, held.result, bucket_bias.T.shape, shards)
+        return (
+            out.result[None],
+            out.d_tokens[None],
+            out.d_memory[None],
+            out.norm_self,
+            out.self_query,
+            out.self_keyval,
+            out.self_output,
+            out.bucket_bias.T,
+            out.norm_cross,
+            out.cross_query,
+            out.cross_keyval,
+            out.cross_output,
+            out.norm_feed,
+            out.feed_in,
+            out.feed_out,
         )
-        made = backward(tokens[0], cotangent[0], onehot.astype(BF16), held, reps, shards)
-        sums = made.fin.transpose(0, 2, 1, 3).reshape(-1, model_width // shards, model_width)
-        sums = sums.astype(F32)
-        parts = feed_in.shape[1] // model_width
-        inner = jnp.concatenate([sums[j] for j in range(parts)], axis=1)
-        outer = sums[parts : 2 * parts].reshape(-1, model_width)
-        co, ck, cv, cq, so, sk, sv, sq = (sums[2 * parts + i] for i in range(8))
-        mine = lambda a, size: lax.dynamic_slice_in_dim(a, shard * size, size, a.ndim - 1)
-        gains = mine(made.small_out[:3, :model_width], model_width // shards)
-        table = mine(made.small_out[8 : 8 + heads, :bucket_count], bucket_count // shards)
-        totals = (gains[0], sq, jnp.stack([sk, sv]), so, table)
-        totals += (gains[1], cq, jnp.stack([ck, cv]), co, gains[2], inner, outer)
-        return (held.result[None], made.d_tokens[None], made.d_memory[None]) + totals
 
     inputs = tokens[0].astype(F32)
     encoded_whole = gather(encoded[0])
@@ -1463,6 +1608,9 @@
     )
     inner, outer = gather(feed_in), gather(feed_out)
 
+    window_buckets = lax.dynamic_slice_in_dim(
+        jnp.pad(buckets, (1, 0)), length - row_anchor - positions, window_width
+    )
     onehot = window_buckets[None, :] == jnp.arange(bucket_count, dtype=jnp.int32)[:, None]
     window = dot(table, onehot.astype(BF16)).reshape(heads // 2, 2, window_width)
 

time: 311 us -> 271 us (0.87)
  local copies, waits for them, and re-layouts: 24.8 us -> 1.37 us
  Pallas kernels: 272 us -> 263 us
  other arithmetic: 6.69 us -> 0 us
    pallas_call x1, Pallas kernels: 173 us -> 157 us  [backward(): pl.pallas_call(functools.partial(backward_kernel, reps, shards, names), i...]
    unnamed x22 -> x0, local copies, waits for them, and re-layouts: 8.5 us -> none
    slice x14 -> x0, local copies, waits for them, and re-layouts: 8.35 us -> none  [the longest x5 2.24 us: layer(): inner = jnp.concatenate([sums[j] for j in range(parts)], axis=1)]
    pallas_call x0 -> x1, Pallas kernels: none -> 8.3 us  [finish(): pl.pallas_call(functools.partial(finish_kernel, squares, shards, names +...]
    convert_element_type x4 -> x0, other arithmetic: 4.99 us -> none  [the longest x1 3.51 us: layer(): sums = sums.astype(F32)]
    another operation x5 -> x0, local copies, waits for them, and re-layouts: 4.19 us -> none  [the longest x3 1.98 us: layer(): small = place(small, jnp.stack([norm_self, norm_cross, norm_feed]), 0)]
where the time goes in v2:
time: 271 us; the launch traced here: 266 us
  Pallas kernels  263 us (97%)
    pallas_call x1, Pallas kernels, backward(): pl.pallas_call(functools.partial(backward_kernel, reps, shards, names), i...  157 us
    pallas_call x1, Pallas kernels, forward(): pl.pallas_call(functools.partial(forward_kernel, reps, shards, tuple(name...  97.5 us
    pallas_call x1, Pallas kernels, finish(): pl.pallas_call(functools.partial(finish_kernel, squares, shards, names +...  8.3 us

profile of v2, /device:TPU:0, one launch (start us, length us, event | category | flops | bytes accessed | tf_op | source)
XLA Modules:
  0.0 265.7 jit_solution(16700385491308154709)
XLA Ops:
  0.6 1.4 pad.4
  2.0 97.5 %shard_map.280 = (bf16[256,768]{1,0:T(8,128)(2,1)}, f32[256,768]{1,0:T(8,128)}, f32[256,768]{1,0:T(8,128)}, f32[2,6,256,128]{3,2,1,0:T(8,128)}, bf16[2,6,256,128...) custom-call(bf16[256,768]{1,0:T(8,128)(2,1)} %bitcast.9, ...), custom_call_target="tpu_custom_call" | custom-call | tf_op jit(solution)/shard_map/pallas_call | solution.py:983
  99.5 157.4 %shard_map.281 = (f32[256,768]{1,0:T(8,128)}, f32[256,768]{1,0:T(8,128)}, f32[24,768]{1,0:T(8,128)}, bf16[16,2,192,384]{3,2,1,0:T(8,128)(2,1)}) custom-call(bf16[256,768]{1,0:T(8,128)(2,1)} %bitcast.10, bf16[256,768]{1,0:T(8,128)(2,1)} %bitcast.11, s32[1,2048]{1,0:T(1,128)} %bitcast.14, f32[24,1024]{1,0:T(8,128)} %get-tuple-element.50.refs_3_, ...), custom_call_target="tpu_custom_call" | custom-call | tf_op jit(solution)/shard_map/pallas_call | solution.py:1440
  257.0 8.3 %shard_map.282 = (f32[192,3072]{1,0:T(8,128)}, f32[768,768]{1,0:T(8,128)}, f32[192,768]{1,0:T(8,128)}, f32[2,192,768]{2,1,0:T(8,128)}, f32[192,768]{1,0:T(8,128)...) custom-call(bf16[16,2,192,384]{3,2,1,0:T(8,128)(2,1)} %get-tuple-ele, ...), custom_call_target="tpu_custom_call" | custom-call | tf_op jit(solution)/shard_map/pallas_call | solution.py:1516

commit v3 on v2

--- a/solution.py
+++ b/solution.py
@@ -18,6 +18,13 @@
 VMEM_LIMIT = 56 * 2**20
 FUSED_LIMIT = 62 * 2**20
 AHEAD = 2
+AHEAD_BUSY = 2
+LAST_SUM = 12
+TICKS = {0: 1, 2: 2, 6: 3, 7: 4, 8: 5, 11: 6, 14: 7, 15: 8, 16: 9}
+LINE = 3
+SELF_PUMPS = ((1, 6), (3, 7), (5, 8))
+CROSS_PUMPS = ((1, 12), (3, 13), (5, 14))
+QUARTERS = (0, 1, 2, 3)
 LATE = (1, 3)
 LATE_START = (-1, 1)
 SLOTS = 4
@@ -287,6 +294,8 @@
 
 
 def added(*parts):
+    if len(parts) == 2:
+        return parts[0] + parts[1]
     total = parts[0].astype(F32)
     for part in parts[1:]:
         total = total + part.astype(F32)
@@ -496,24 +505,44 @@
 
     @staticmethod
     def scratch(units, nx):
-        copies = 1 + 4 * (nx - 1)
+        copies = 1 + 8 * (nx - 1)
         return [
             pltpu.SemaphoreType.DMA((units, copies)),
             pltpu.SemaphoreType.DMA((units, copies)),
             pltpu.SemaphoreType.DMA((units,)),
         ]
 
-    def rows(self, u, shard, half=None):
-        if isinstance(u, int) and u >= self.square:
-            at = self.square * self.width + shard * self.hidden_rows + (u - self.square) * self.q
+    def cut(self, u, far_first, far_second=False):
+        p = self.place
+        first, second = (p.y, p.low) if u % 2 == 0 else (p.low, p.y)
+        first = 1 - first if far_first else first
+        second = 1 - second if far_second else second
+        if u not in QUARTERS:
+            return first * (self.q // 2)
+        return (first * 2 + second) * (self.q // 4)
+
+    def size(self, u):
+        return self.q // 4 if u in QUARTERS else self.q // 2
+
+    def first(self, u):
+        return self.place.other_y() if u % 2 == 0 else self.place.other_low()
+
+    def second(self, u):
+        return self.place.other_low() if u % 2 == 0 else self.place.other_y()
+
+    def part(self, u, shard, at=None):
+        if u >= self.square:
+            start = self.square * self.width + shard * self.hidden_rows
+            start = start + (u - self.square) * self.q
         else:
-            at = u * self.width + shard * self.q
-        if half is None:
-            return pl.ds(pl.multiple_of(at, 16), self.q)
-        return pl.ds(pl.multiple_of(at + half * (self.q // 2), 16), self.q // 2)
-
-    def part(self, u, shard, half=None):
-        return self.whole.at[self.rows(u, shard, half)]
+            start = u * self.width + shard * self.q
+        if at is None:
+            return self.whole.at[pl.ds(pl.multiple_of(start, 16), self.q)]
+        return self.whole.at[pl.ds(pl.multiple_of(start + at, 16), self.size(u))]
+
+    def came(self, d):
+        p = self.place
+        return lax.rem(p.x + p.nx - d, p.nx) * 2 + p.core
 
     def copy(self, u, which, src, dst, device):
         return remote(src, dst, self.send.at[u, which], self.recv.at[u, which], device)
@@ -529,27 +558,26 @@
 
     def over_x(self, u, d):
         p = self.place
-        half = self.own[u].at[pl.ds(pl.multiple_of(p.y * (self.q // 2), 16), self.q // 2)]
-        return self.copy(u, 4 * d - 3, half, self.part(u, p.shard, p.y), p.x_at(d)[1])
-
-    def came(self, d):
-        p = self.place
-        return lax.rem(p.x + p.nx - d, p.nx) * 2 + p.core
-
-    def on_y(self, u, d):
-        p = self.place
-        here = self.part(u, self.came(d), p.y)
-        return self.copy(u, 4 * d - 2, here, here, p.other_y())
-
-    def on_core(self, u, d):
-        p = self.place
-        here = self.part(u, self.came(d), p.y)
-        return self.copy(u, 4 * d - 1, here, here, p.other_core())
-
-    def last_core(self, u, d):
-        p = self.place
-        here = self.part(u, self.came(d), 1 - p.y)
-        return self.copy(u, 4 * d, here, here, p.other_core())
+        at = self.cut(u, False)
+        src = self.own[u].at[pl.ds(pl.multiple_of(at, 16), self.size(u))]
+        return self.copy(u, 8 * d - 7, src, self.part(u, p.shard, at), p.x_at(d)[1])
+
+    def on(self, u, d, which, far_first, far_second, device):
+        here = self.part(u, self.came(d), self.cut(u, far_first, far_second))
+        return self.copy(u, 8 * d - 7 + which, here, here, device)
+
+    def onward(self, u, d, which):
+        core, first, second = self.place.other_core(), self.first(u), self.second(u)
+        far_first, far_second, device = (
+            (False, False, first),
+            (False, False, second),
+            (False, False, core),
+            (False, True, first),
+            (False, True, core),
+            (True, False, core),
+            (True, True, core),
+        )[which]
+        return self.on(u, d, which + 1, far_first, far_second, device)
 
     def issue(self, u):
         for d in range(1, self.place.nx):
@@ -559,39 +587,37 @@
 
     def relay_x(self, u):
         for d in range(1, self.place.nx):
-            self.arrive_x(u, d)
-            self.on_y(u, d).start()
-            self.on_core(u, d).start()
-
-    def arrive_x(self, u, d):
-        p = self.place
-        here = self.part(u, self.came(d), p.y)
-        self.copy(u, 4 * d - 3, here, here, p.x_at(d)[1]).wait_recv()
-
-    def relay_y(self, u):
+            self.over_x(u, d).wait_recv()
+            for which in (0, 1, 2) if u in QUARTERS else (0, 2):
+                self.onward(u, d, which).start()
+
+    def relay_second(self, u):
+        for d in range(1, self.place.nx if u in QUARTERS else 1):
+            self.onward(u, d, 1).wait_recv()
+            self.onward(u, d, 3).start()
+            self.onward(u, d, 4).start()
+
+    def relay_first(self, u):
         for d in range(1, self.place.nx):
-            self.on_y(u, d).wait_recv()
-            self.last_core(u, d).start()
+            self.onward(u, d, 0).wait_recv()
+            self.onward(u, d, 5).start()
+            if u in QUARTERS:
+                self.onward(u, d, 3).wait_recv()
+                self.onward(u, d, 6).start()
 
     def ready(self, u):
-        p = self.place
-        here = self.part(u, p.shard)
-        pltpu.make_async_copy(here, here, self.own_sem.at[u]).wait()
-        self.copy(u, 0, here, here, p.other_core()).wait_recv()
-        for d in range(1, p.nx):
-            self.on_core(u, d).wait_recv()
-            self.last_core(u, d).wait_recv()
+        self.keep(u).wait()
+        self.to_core(u).wait_recv()
+        for d in range(1, self.place.nx):
+            for which in (2, 4, 5, 6) if u in QUARTERS else (2, 5):
+                self.onward(u, d, which).wait_recv()
 
     def sent(self, u):
-        p = self.place
-        here = self.part(u, p.shard)
-        self.copy(u, 0, here, here, p.other_core()).wait_send()
-        for d in range(1, p.nx):
-            here = self.part(u, self.came(d), p.y)
-            self.copy(u, 4 * d - 3, here, here, p.x_at(d)[1]).wait_send()
-            self.on_y(u, d).wait_send()
-            self.on_core(u, d).wait_send()
-            self.last_core(u, d).wait_send()
+        self.to_core(u).wait_send()
+        for d in range(1, self.place.nx):
+            self.over_x(u, d).wait_send()
+            for which in range(7) if u in QUARTERS else (0, 2, 5):
+                self.onward(u, d, which).wait_send()
 
 
 class Spread:
@@ -711,6 +737,13 @@
     def emit_kv(i):
         return pltpu.make_async_copy(r.kv.at[i], r.kv_out.at[i], r.out_sem.at[units + i])
 
+    leaving = []
+
+    def emit(src, dst):
+        copy = pltpu.make_async_copy(src, dst, r.emit_sem.at[len(leaving)])
+        copy.start()
+        leaving.append(copy)
+
     emit_tok = pltpu.make_async_copy(r.tok_t, r.tok_out, r.out_sem.at[units + 4])
     emit_enc = pltpu.make_async_copy(r.enc_t, r.enc_out, r.out_sem.at[units + 5])
 
@@ -738,18 +771,37 @@
     r.row_ids[...] = jnp.broadcast_to(ids, (8, rows)).T[:, 0:1]
     enter(place)
     small.launch()
-    line = [(gather, (u,)) for u in (1, 2, 0)] + [(tokens, ()), (memories, ())]
-    line += [(gather, (u,)) for u in [3, 5, 6, 4, 7] + list(range(8, units))]
+    line = [(gather, (u,)) for u in (1, 2, 0, 3)] + [(tokens, ())]
+    line += [(gather, (u,)) for u in (5, 6)] + [(memories, ())]
+    line += [(gather, (u,)) for u in [4, 7] + list(range(8, units))]
+    pumped = [0]
+    steps = ("relay_x", "relay_second", "relay_first")
 
     def issue(at):
         if at < len(line):
             line[at][0].issue(*line[at][1])
 
-    def relay(owner, *u):
-        owner.relay_x(*u)
-        issue(line.index((owner, u)) + AHEAD)
-
-    for at in range(AHEAD):
+    def pump(at):
+        for late, name in enumerate(steps):
+            if 0 <= at - late < len(line):
+                owner, u = line[at - late]
+                if hasattr(owner, name):
+                    getattr(owner, name)(*u)
+            if late == 0:
+                issue(at + LINE)
+
+    def pump_to(end):
+        while pumped[0] < end:
+            pump(pumped[0])
+            pumped[0] += 1
+
+    def have(*wanted):
+        last = max(line.index((gather, (u,))) for u in wanted)
+        pump_to(last + len(steps))
+        for u in wanted:
+            gather.ready(u)
+
+    for at in range(LINE):
         issue(at)
     small.step(0, 2)
     gathered = small.step(1, 2)
@@ -758,11 +810,7 @@
     biases = dot(table, bucket_onehot(r.buckets, place, rows, length).astype(BF16))
     for i in range(pairs):
         r.window[i] = biases[2 * i : 2 * i + 2]
-    for u in (1, 2, 0):
-        relay(gather, u)
-    for u in (1, 2, 0):
-        gather.relay_y(u)
-    relay(tokens)
+    pump_to(5)
     tokens.ready()
     tokens.sent()
 
@@ -794,7 +842,7 @@
     def project_query(normed, u, which):
         out = dot(normed, weight(u)).astype(BF16)
         for j in range(pairs):
-            r.q_out[which, j] = out[:, j * LANES : (j + 1) * LANES]
+            r.queries[which, j] = out[:, j * LANES : (j + 1) * LANES]
 
     def attention(which, bias, relays):
         def pair(i, carry):
@@ -806,59 +854,43 @@
             more = None
             if bias:
                 more = (r.row_ids[...], r.small_held[2, 3:4, :length], r.window[i])
-            r.low_out[which, i] = attend_pair(
-                r.q_out[which, i],
+            r.low[which, i] = attend_pair(
+                r.queries[which, i],
                 r.kv[2 * which, i],
                 r.kv.at[2 * which + 1, i],
                 r.probs.at[slot],
                 more,
             )
             emit_p(which, i).start()
-            for step, relay, u in relays:
+            for step, end in relays:
                 @pl.when(i == step)
                 def _():
-                    relay(*u)
+                    pump_to(end)
 
             return carry
 
         lax.fori_loop(0, pairs, pair, 0)
         emit_p(which, 0).wait()
         emit_p(which, 1).wait()
-        low = [r.low_out[which, j].astype(BF16) for j in range(pairs)]
+        low = [r.low[which, j].astype(BF16) for j in range(pairs)]
         low = jnp.concatenate(low, axis=1)
         r.low_t[which] = low.T
+        emit(r.low.at[which], r.low_out.at[which])
+        emit(r.low_t.at[which], r.low_t_out.at[which])
+        emit(r.queries.at[which], r.q_out.at[which])
         return low
 
-    gather.ready(1)
-    gather.ready(2)
+    have(1, 2)
     project_pair(r.tok, 0, 1)
-    gather.ready(0)
+    have(0)
     emit_weights(0, 3).start()
     mine = pl.ds(pl.multiple_of(place.shard * rows, 16), rows)
     project_query(r.tok[mine, :], 0, 0)
-    over_y = gather.relay_y
-
-    def over_x(u):
-        relay(gather, u)
-
-    low = attention(
-        0,
-        True,
-        [
-            (0, relay, (memories,)),
-            (1, over_x, (3,)),
-            (2, over_x, (5,)),
-            (3, over_x, (6,)),
-            (3, over_y, (3,)),
-            (4, over_x, (4,)),
-            (4, over_y, (5,)),
-            (5, over_y, (6,)),
-        ],
-    )
-    gather.ready(3)
-    r.first_out[...] = r.tok_in[...].astype(F32) + dot(low, weight(3))
-    over_x(7)
-    over_y(4)
+    low = attention(0, True, SELF_PUMPS)
+    have(3)
+    r.first[...] = r.tok_in[...].astype(F32) + dot(low, weight(3))
+    emit(r.first, r.first_out)
+    pump_to(8)
     memories.ready()
 
     def turn_rows(i, carry):
@@ -868,50 +900,35 @@
 
     lax.fori_loop(0, length // rows, turn_rows, 0)
     emit_enc.start()
-    gather.ready(5)
-    gather.ready(6)
+    have(5, 6)
     project_pair(r.enc, 2, 5)
-    gather.ready(4)
-    first = r.first_out[...]
+    have(4)
+    first = r.first[...]
     normed = (first * rms_scale(first) * gain(1)).astype(BF16)
     r.normed2_t[...] = normed.T
+    emit(r.normed2_t, r.normed2_out)
     project_query(normed, 4, 1)
-    over_x(8)
-    over_y(7)
-    low = attention(
-        1,
-        False,
-        [
-            (1, over_x, (9,)),
-            (1, over_y, (8,)),
-            (2, over_x, (10,)),
-            (3, over_y, (9,)),
-            (4, over_x, (11,)),
-            (5, over_y, (10,)),
-        ],
-    )
-    gather.ready(7)
+    low = attention(1, False, CROSS_PUMPS)
+    have(7)
     emit_weights(3, 5).start()
-    r.second_out[...] = r.first_out[...] + dot(low, weight(7))
-    over_x(12)
-    over_y(11)
-    second = r.second_out[...]
+    r.second[...] = r.first[...] + dot(low, weight(7))
+    emit(r.second, r.second_out)
+    second = r.second[...]
     normed = (second * rms_scale(second) * gain(2)).astype(BF16)
     r.normed[...] = normed
     r.normed3_t[...] = normed.T
+    emit(r.normed3_t, r.normed3_out)
     for j in range(part):
-        gather.ready(8 + j)
+        have(8 + j)
         value, slope = gelu_parts(dot(r.normed[...], weight(8 + j)))
         value = value.astype(BF16)
         r.hidden[j] = value
         r.hidden_t[j * width : (j + 1) * width, :] = value.T
-        r.slope_out[j] = slope
-        if j + 1 < part:
-            over_x(13 + j)
-            over_y(12 + j)
-    over_y(units - 1)
-    for j in range(part):
-        gather.ready(8 + part + j)
+        r.slope[j] = slope
+        block = pl.ds(j * width, width)
+        emit(r.hidden_t.at[block], r.hidden_out.at[block])
+        emit(r.slope.at[j], r.slope_out.at[j])
+    have(*range(8 + part, units))
     emit_weights(8, units - 8).start()
     total = second
     for j in range(part):
@@ -927,6 +944,8 @@
         emit_kv(i).wait()
     emit_tok.wait()
     emit_enc.wait()
+    for copy in leaving:
+        copy.wait()
 
 
 def forward(tokens, encoded, ids, buckets, gains, bucket_bias, shards_of, reps, shards):
@@ -942,16 +961,16 @@
     near = lambda *shape, dtype=F32: (pl.BlockSpec(memory_space=pltpu.VMEM), jax.ShapeDtypeStruct(shape, dtype))
     outs = dict(
         result=near(rows, width, dtype=BF16),
-        first_out=near(rows, width),
-        second_out=near(rows, width),
-        low_out=near(2, pairs, rows, LANES),
-        q_out=near(2, pairs, rows, LANES, dtype=BF16),
         small_out=near(*small),
-        low_t=near(2, width, rows, dtype=BF16),
-        normed2_t=near(width, rows, dtype=BF16),
-        normed3_t=near(width, rows, dtype=BF16),
-        hidden_t=near(hidden, rows, dtype=BF16),
-        slope_out=near(hidden // width, rows, width),
+        first_out=kept(rows, width, dtype=F32),
+        second_out=kept(rows, width, dtype=F32),
+        low_out=kept(2, pairs, rows, LANES, dtype=F32),
+        low_t_out=kept(2, width, rows),
+        q_out=kept(2, pairs, rows, LANES),
+        normed2_out=kept(width, rows),
+        normed3_out=kept(width, rows),
+        hidden_out=kept(hidden, rows),
+        slope_out=kept(hidden // width, rows, width, dtype=F32),
         w_out=kept(units * width, width),
         kv_out=kept(4, pairs, length, LANES),
         tok_out=kept(width, length),
@@ -966,6 +985,16 @@
         window=pltpu.VMEM((pairs, 2, length + rows), F32),
         row_ids=pltpu.VMEM((rows, 1), F32),
         probs=pltpu.VMEM((2, 2 * rows, length), BF16),
+        first=pltpu.VMEM((rows, width), F32),
+        second=pltpu.VMEM((rows, width), F32),
+        low=pltpu.VMEM((2, pairs, rows, LANES), F32),
+        low_t=pltpu.VMEM((2, width, rows), BF16),
+        queries=pltpu.VMEM((2, pairs, rows, LANES), BF16),
+        normed2_t=pltpu.VMEM((width, rows), BF16),
+        normed3_t=pltpu.VMEM((width, rows), BF16),
+        hidden_t=pltpu.VMEM((hidden, rows), BF16),
+        slope=pltpu.VMEM((hidden // width, rows, width), F32),
+        emit_sem=pltpu.SemaphoreType.DMA((10 + 2 * (hidden // width),)),
         normed=pltpu.VMEM((rows, width), BF16),
         hidden=pltpu.VMEM((hidden // width, rows, width), BF16),
         tok_t=pltpu.VMEM((width, length), BF16),
@@ -1035,7 +1064,7 @@
         p = self.place
         for d in range(1, p.nx):
             self.over_x(d).wait_recv()
-        return added(self.recv_a[p.x], *[self.recv_b[d] for d in range(p.nx - 1)])
+        return added(self.recv_a[p.x], *[self.recv_b[d] for d in range(p.nx - 1)]).astype(F32)
 
     def sent(self):
         for d in range(1, self.place.nx):
@@ -1074,6 +1103,7 @@
     return d_query, d_keys, d_values, windows
 
 
+BROUGHT = ("normed3_t", "hidden_t", "second", "low_t", "queries", "low", "first", "normed2_t")
 REDUCTION = ("_parts", "_x", "_y", "_low", "_high", "_send", "_recv", "_own")
 
 
@@ -1112,6 +1142,13 @@
         block = pl.ds(u * width, width)
         return pltpu.make_async_copy(r.w_in.at[block], r.w.at[slot], r.w_sem.at[slot])
 
+    ticks = [0]
+
+    def slot_done(slot):
+        while ticks[0] < TICKS.get(slot, 0):
+            advance(ticks[0])
+            ticks[0] += 1
+
     def load_slope(j):
         slot = j % 2
         return pltpu.make_async_copy(r.slope.at[j], r.slopes.at[slot], r.s_sem.at[slot])
@@ -1149,15 +1186,22 @@
         if n >= SLOTS:
             left(n - SLOTS)
 
+    done_stages = {n: 0 for n in range(units)}
+    started = [0]
+
+    def set_out(end):
+        while started[0] < min(end, len(order)):
+            red, u = owner(order[started[0]])
+            red.start(u, 0)
+            started[0] += 1
+
     def take(n):
         red, u = owner(n)
         red.collect(u, away(n), r.made.at[n % SLOTS, place.core])
         if n in late:
             red.start(u, 0)
-        elif order.index(n) < AHEAD:
-            red.start(u, 0)
-
-    done_stages = {n: 0 for n in range(units)}
+        elif order.index(n) < AHEAD_BUSY:
+            set_out(order.index(n) + 1)
 
     def move(n, upto):
         red, u = owner(n)
@@ -1170,16 +1214,23 @@
             at = t - back
             if 0 <= at < len(order):
                 move(order[at], back + 1)
-            if back == 0 and 0 <= t + AHEAD < len(order):
-                red, u = owner(order[t + AHEAD])
-                red.start(u, 0)
+            if back == 0:
+                set_out(t + 1 + (AHEAD_BUSY if t + 1 < max(TICKS.values()) else AHEAD))
         for i, n in enumerate(late):
             move(n, t - LATE_START[i])
 
-    enter(place)
+    def bring(name):
+        source, sem = getattr(r, name + "_in"), r.bring_sem.at[BROUGHT.index(name)]
+        return pltpu.make_async_copy(source, getattr(r, name), sem)
+
     load_slope(0).start()
     for slot, u in enumerate((8, 8 + part)):
         load_weight(u, slot).start()
+    for name in BROUGHT[:3]:
+        bring(name).start()
+    enter(place)
+    for name in BROUGHT[3:]:
+        bring(name).start()
     for slot in range(2):
         load_kv(2 + slot, slot).start()
         load_p(1, slot).start()
@@ -1195,6 +1246,8 @@
             load_slope(j + 1).start()
             load_weight(8 + j + 1, 2 - slot).start()
             load_weight(8 + part + j + 1, 3 - slot).start()
+        if j == 0:
+            bring("normed3_t").wait()
         grad_hidden = dot_nt(r.cotangent[...], r.w[slot + 1])
         grad = (grad_hidden * r.slopes[j % 2]).astype(BF16)
         free(j)
@@ -1205,6 +1258,7 @@
     for slot, u in ((0, 7), (1, 5), (2, 6), (3, 4)):
         load_weight(u, slot).start()
     take(part - 1)
+    bring("hidden_t").wait()
     for m in range(part):
         n = part + m
         free(n)
@@ -1218,12 +1272,13 @@
         fill(n, value)
         if m >= 1:
             take(n - 1)
+    bring("second").wait()
     back, d_gain3 = rms_back(r.second[...], gain(2), r.acc[...])
     r.grad[...] = r.cotangent[...].astype(F32) + back
     take(2 * part - 1)
-    advance(0)
-
-    def attention(which, fold, steps):
+    slot_done(0)
+
+    def attention(which, fold, first_slot):
         def pair(i, carry):
             slot = lax.rem(i, 2)
             load_p(which, i).wait()
@@ -1248,10 +1303,11 @@
             def _():
                 load_p(which, i + 2).start()
 
-            for step, n in steps:
-                @pl.when(i == step)
-                def _():
-                    advance(n)
+            for step in range(pairs):
+                if first_slot + step in TICKS:
+                    @pl.when(i == step)
+                    def _():
+                        slot_done(first_slot + step)
 
             return carry
 
@@ -1264,6 +1320,8 @@
     def joined_query():
         return jnp.concatenate([r.d_query[i] for i in range(pairs)], axis=1)
 
+    for name in BROUGHT[3:]:
+        bring(name).wait()
     n = 2 * part
     grad_low = r.grad[...].astype(BF16)
     free(n)
@@ -1274,7 +1332,7 @@
     take(n)
     for slot in range(2):
         load_kv(2 + slot, slot).wait()
-    attention(1, False, [(1, 1), (5, 2)])
+    attention(1, False, 1)
     for slot in range(2):
         load_kv(slot, slot).start()
         load_p(0, slot).start()
@@ -1290,7 +1348,7 @@
     free(n + 2)
     fill(n + 2, dot_nt(r.rows_t[...], r.dv_t[...]))
     take(n + 1)
-    advance(3)
+    slot_done(7)
     load_t(r.tok_t, 1).start()
     d_query = joined_query()
     load_weight(4, 3).wait()
@@ -1300,7 +1358,7 @@
     fill(n + 3, dot(r.normed2_t[...], d_query))
     take(n + 2)
     r.grad[...] = r.grad[...] + back
-    advance(4)
+    slot_done(8)
 
     grad_low = r.grad[...].astype(BF16)
     take(n + 3)
@@ -1311,7 +1369,7 @@
     take(n + 4)
     for slot in range(2):
         load_kv(slot, slot).wait()
-    attention(0, True, [(2, 5), (5, 6)])
+    attention(0, True, 9)
     load_weight(1, 1).wait()
     load_weight(2, 2).wait()
     sum_memory.to_core().wait_send()
@@ -1324,7 +1382,7 @@
     fill(n + 6, dot_nt(r.rows_t[...], r.dv_t[...]))
     take(n + 5)
     r.d_memory[...] = sum_memory.finish().T
-    advance(7)
+    slot_done(15)
     d_query = joined_query()
     free(n + 7)
     mine = pl.ds(pl.multiple_of(place.shard * rows, LANES), rows)
@@ -1341,19 +1399,21 @@
         preferred_element_type=F32,
     )
     take(n + 7)
-    advance(8)
-    values = r.tokens[...].astype(F32)
-    back, d_gain1 = rms_back(values, gain(0), r.acc[...] + sum_tokens.finish().T)
-    r.d_tokens[...] = r.grad[...] + back
-    r.small_held[0] = jnp.zeros(r.small_held.shape[1:], F32)
-    for i, d_gain in enumerate((d_gain1, d_gain2, d_gain3)):
-        r.small_held[0, i : i + 1, :width] = d_gain
-    r.small_held[0, 8 : 8 + 2 * pairs, :LANES] = d_table
-    small.launch()
-    for t in range(9, len(order) + stages):
+    slot_done(16)
+    for t in range(ticks[0], len(order) + stages):
         advance(t)
-        if t < 14:
-            small.step(t - 9)
+        if t == LAST_SUM:
+            values = r.tokens[...].astype(F32)
+            total = r.acc[...] + sum_tokens.finish().T
+            back, d_gain1 = rms_back(values, gain(0), total)
+            r.d_tokens[...] = r.grad[...] + back
+            r.small_held[0] = jnp.zeros(r.small_held.shape[1:], F32)
+            for i, d_gain in enumerate((d_gain1, d_gain2, d_gain3)):
+                r.small_held[0, i : i + 1, :width] = d_gain
+            r.small_held[0, 8 : 8 + 2 * pairs, :LANES] = d_table
+            small.launch()
+        elif LAST_SUM < t < LAST_SUM + 6:
+            small.step(t - LAST_SUM - 1)
     for n in range(units):
         move(n, stages)
     r.small_out[...] = r.small_held[5]
@@ -1378,19 +1438,15 @@
     small = (24, width)
     kept = pl.BlockSpec(memory_space=pl.ANY)
     near = pl.BlockSpec(memory_space=pltpu.VMEM)
+    arrays = (held.normed3_out, held.hidden_out, held.second_out, held.low_t_out)
+    arrays += (held.q_out, held.low_out, held.first_out, held.normed2_out)
+    brought = dict(zip(BROUGHT, arrays))
     ins = dict(
         tokens=(near, tokens),
         cotangent=(near, cotangent),
         buckets=(near, buckets),
         gains=(near, held.small_out),
-        first=(near, held.first_out),
-        second=(near, held.second_out),
-        low=(near, held.low_out),
-        low_t=(near, held.low_t),
-        queries=(near, held.q_out),
-        normed2_t=(near, held.normed2_t),
-        normed3_t=(near, held.normed3_t),
-        hidden_t=(near, held.hidden_t),
+        **{name + "_in": (kept, array) for name, array in brought.items()},
         slope=(kept, held.slope_out),
         tok_t=(kept, held.tok_out),
         enc_t=(kept, held.enc_out),
@@ -1404,7 +1460,9 @@
         small_out=(near, jax.ShapeDtypeStruct(small, F32)),
         fin=(kept, jax.ShapeDtypeStruct((units, 2, q, half), BF16)),
     )
-    scratch = dict(
+    scratch = {name: pltpu.VMEM(array.shape, array.dtype) for name, array in brought.items()}
+    scratch.update(
+        bring_sem=pltpu.SemaphoreType.DMA((len(brought),)),
         w=pltpu.VMEM((4, width, width), BF16),
         kv=pltpu.VMEM((2, pairs, length, LANES), BF16),
         probs=pltpu.VMEM((2, 2 * rows, length), BF16),

time: 271 us -> 257 us (0.948)
  Pallas kernels: 263 us -> 250 us
    pallas_call x1, Pallas kernels: 97.5 us -> 87.9 us  [forward(): pl.pallas_call(functools.partial(forward_kernel, reps, shards, tuple(name...]
    pallas_call x1, Pallas kernels: 157 us -> 153 us  [backward(): pl.pallas_call(functools.partial(backward_kernel, reps, shards, names), i...]
where the time goes in v3:
time: 257 us; the launch traced here: 252 us
  Pallas kernels  250 us (97%)
    pallas_call x1, Pallas kernels, backward(): pl.pallas_call(functools.partial(backward_kernel, reps, shards, names), i...  153 us
    pallas_call x1, Pallas kernels, forward(): pl.pallas_call(functools.partial(forward_kernel, reps, shards, tuple(name...  87.9 us
    pallas_call x1, Pallas kernels, finish(): pl.pallas_call(functools.partial(finish_kernel, squares, shards, names +...  8.3 us

profile of v3, /device:TPU:0, one launch (start us, length us, event | category | flops | bytes accessed | tf_op | source)
XLA Modules:
  0.0 252.2 jit_solution(9306745402461365928)
XLA Ops:
  0.6 1.4 pad.4
  2.0 87.9 %shard_map.280 = (bf16[256,768]{1,0:T(8,128)(2,1)}, f32[24,1024]{1,0:T(8,128)}, f32[256,768]{1,0:T(8,128)}, f32[256,768]{1,0:T(8,128)}, f32[2,6,256,128]{3,2,1,0...) custom-call(bf16[256,768]{1,0:T(8,128)(2,1)} %bitcast.9, ...), custom_call_target="tpu_custom_call" | custom-call | tf_op jit(solution)/shard_map/pallas_call | solution.py:1012
  90.0 153.5 %shard_map.281 = (f32[256,768]{1,0:T(8,128)}, f32[256,768]{1,0:T(8,128)}, f32[24,768]{1,0:T(8,128)}, bf16[16,2,192,384]{3,2,1,0:T(8,128)(2,1)}) custom-call(bf16[256,768]{1,0:T(8,128)(2,1)} %bitcast.10, bf16[256,768]{1,0:T(8,128)(2,1)} %bitcast.11, s32[1,2048]{1,0:T(1,128)} %bitcast.14, f32[24,1024]{1,0:T(8,128)} %get-tuple-element.50.refs_3_, ...), custom_call_target="tpu_custom_call" | custom-call | tf_op jit(solution)/shard_map/pallas_call | solution.py:1498
  243.4 8.3 %shard_map.282 = (f32[192,3072]{1,0:T(8,128)}, f32[768,768]{1,0:T(8,128)}, f32[192,768]{1,0:T(8,128)}, f32[2,192,768]{2,1,0:T(8,128)}, f32[192,768]{1,0:T(8,128)...) custom-call(bf16[16,2,192,384]{3,2,1,0:T(8,128)(2,1)} %get-tuple-ele, ...), custom_call_target="tpu_custom_call" | custom-call | tf_op jit(solution)/shard_map/pallas_call | solution.py:1574
